TPU v7x, 512 devices: a whole 4x4x16 slice. The times are simulated.
512 devices in a mesh: gx: 32 (over x, y, core), gy: 16 (over z).
Axes of the slice: x: 4, y: 4, z: 16, core: 2. Of those that a mesh axis runs over, the one named last changes fastest.
Arguments:
- state: float32 [5, 512, 128, 128], P(None, 'gx', 'gy'), may hold values from -4 to 4
- pinning: float32 [512, 128, 128], P('gx', 'gy'), may hold values from -1 to 1
- lead_values: float32 [2, 128, 128], P(None, 'gy'), may hold values from -4 to 4
Outputs:
- next_state: float32 [5, 512, 128, 128], P(None, 'gx', 'gy')
- potential: float32 [512, 128, 128], P('gx', 'gy')
All inputs are finite; a program needn't handle non-finite values.
Results may differ from a plain program's by a relative error of at most 0.0003.
Values sent between devices are 32-bit elements; how exact they have to be, the bound alone decides.
A program may use at most 128 MiB of HBM per device.

v0:
```python
import math

import jax
import jax.numpy as jnp
from jax import lax
from jax.sharding import PartitionSpec as P

LEVELS = 4
PRE = 3
POST = 2


OMEGA = 0.8
DT = 0.05
KAPPA2 = 2.0


def extended(cells, sides, width):
    for axis, dim in sides:
        count = lax.axis_size(axis)
        ends = count - 1
        head = lax.slice_in_dim(cells, 0, width, axis=dim)
        tail = lax.slice_in_dim(cells, cells.shape[dim] - width, cells.shape[dim], axis=dim)
        cells = jnp.concatenate(
            [
                lax.ppermute(tail, axis, [(i, (i + 1) % count) for i in range(ends)]),
                cells,
                lax.ppermute(head, axis, [((i + 1) % count, i) for i in range(ends)]),
            ],
            axis=dim,
        )
    return cells


def shifted(block, axis, distance):
    devices = range(lax.axis_size(axis))
    route = [(i - distance, i) for i in devices if i - distance in devices]
    return lax.ppermute(block, axis, route)


def window_of(values, offset):
    ext_x, ext_y, ext_z = values.shape
    return values[
        1 + offset[0] : ext_x - 1 + offset[0],
        1 + offset[1] : ext_y - 1 + offset[1],
        1 + offset[2] : ext_z - 1 + offset[2],
    ]


def unit_step(axis_no):
    return tuple((1 if place == axis_no else 0 for place in range(3)))


def offset_sum(first, second):
    return tuple((a + b for a, b in zip(first, second)))


def negated(offset):
    return tuple((-a for a in offset))


def plaquette(links, first, second, offset):
    ahead_first = offset_sum(offset, unit_step(first))
    ahead_second = offset_sum(offset, unit_step(second))
    return (
        window_of(links[second], ahead_first)
        - window_of(links[second], offset)
        - (window_of(links[first], ahead_second) - window_of(links[first], offset))
    )


def flow_terms(padded, pinning):
    psi_real = padded[0]
    psi_imag = padded[1]
    links = (padded[2], padded[3], padded[4])
    anchor = (0, 0, 0)
    here_re = window_of(psi_real, anchor)
    here_im = window_of(psi_imag, anchor)
    lap_re = jnp.zeros_like(here_re)
    lap_im = jnp.zeros_like(here_re)
    divergence = jnp.zeros_like(here_re)
    currents = []
    for comp in range(3):
        ahead = unit_step(comp)
        behind = negated(ahead)
        cos_ahead = jnp.cos(window_of(links[comp], anchor))
        sin_ahead = jnp.sin(window_of(links[comp], anchor))
        next_re = window_of(psi_real, ahead)
        next_im = window_of(psi_imag, ahead)
        moved_re = cos_ahead * next_re + sin_ahead * next_im
        moved_im = cos_ahead * next_im - sin_ahead * next_re
        cos_behind = jnp.cos(window_of(links[comp], behind))
        sin_behind = jnp.sin(window_of(links[comp], behind))
        prev_re = window_of(psi_real, behind)
        prev_im = window_of(psi_imag, behind)
        back_re = cos_behind * prev_re - sin_behind * prev_im
        back_im = cos_behind * prev_im + sin_behind * prev_re
        into_re = cos_behind * here_re + sin_behind * here_im
        into_im = cos_behind * here_im - sin_behind * here_re
        current_here = here_re * moved_im - here_im * moved_re
        current_back = prev_re * into_im - prev_im * into_re
        lap_re = lap_re + moved_re + back_re
        lap_im = lap_im + moved_im + back_im
        divergence = divergence + (current_here - current_back)
        currents.append(current_here)
    lap_re = lap_re - 6.0 * here_re
    lap_im = lap_im - 6.0 * here_im
    condense = pinning - (here_re * here_re + here_im * here_im)
    rate_re = lap_re + condense * here_re
    rate_im = lap_im + condense * here_im
    step_x = unit_step(0)
    step_y = unit_step(1)
    step_z = unit_step(2)
    curl_x = (
        plaquette(links, 0, 1, anchor)
        - plaquette(links, 0, 1, negated(step_y))
        - (plaquette(links, 2, 0, anchor) - plaquette(links, 2, 0, negated(step_z)))
    )
    curl_y = (
        plaquette(links, 1, 2, anchor)
        - plaquette(links, 1, 2, negated(step_z))
        - (plaquette(links, 0, 1, anchor) - plaquette(links, 0, 1, negated(step_x)))
    )
    curl_z = (
        plaquette(links, 2, 0, anchor)
        - plaquette(links, 2, 0, negated(step_x))
        - (plaquette(links, 1, 2, anchor) - plaquette(links, 1, 2, negated(step_y)))
    )
    rates_link = [
        currents[0] - KAPPA2 * curl_x,
        currents[1] - KAPPA2 * curl_y,
        currents[2] - KAPPA2 * curl_z,
    ]
    return (rate_re, rate_im, rates_link, divergence, here_re, here_im)


def neighbours(padded):
    wider = jnp.pad(padded, ((0, 0), (0, 0), (1, 1)), mode="edge")
    centre = wider[1:-1, 1:-1]
    summed = wider[2:, 1:-1, 1:-1] + wider[:-2, 1:-1, 1:-1]
    summed = summed + wider[1:-1, 2:, 1:-1] + wider[1:-1, :-2, 1:-1]
    summed = summed + centre[:, :, 2:] + centre[:, :, :-2]
    return summed


def level_apply(iterate, around, factor):
    return (6.0 * iterate - around) * factor


def jacobi_sweep(iterate, applied, source, factor):
    return iterate + OMEGA * (source - applied) / (6.0 * factor)


def restrict(values):
    size_x, size_y, size_z = values.shape
    return (
        values.reshape(size_x // 2, 2, size_y // 2, 2, size_z // 2, 2).sum(axis=(1, 3, 5)) * 0.125
    )


def prolong(values):
    return jnp.repeat(jnp.repeat(jnp.repeat(values, 2, 0), 2, 1), 2, 2)


def sine_table(count):
    modes = jnp.arange(1, count + 1, dtype=jnp.float32)
    return jnp.sqrt(2.0 / (count + 1)) * jnp.sin(
        math.pi / (count + 1) * modes[:, None] * modes[None, :]
    )


def sine_values(count):
    modes = jnp.arange(1, count + 1, dtype=jnp.float32)
    return 2.0 - 2.0 * jnp.cos(math.pi / (count + 1) * modes)


def cosine_table(count):
    modes = jnp.arange(count, dtype=jnp.float32)
    cells = jnp.arange(count, dtype=jnp.float32) + 0.5
    weights = jnp.where(modes == 0.0, 1.0, 2.0) / count
    return jnp.sqrt(weights)[:, None] * jnp.cos(math.pi / count * modes[:, None] * cells[None, :])


def cosine_values(count):
    modes = jnp.arange(count, dtype=jnp.float32)
    return 2.0 - 2.0 * jnp.cos(math.pi / count * modes)


def transform(values, table_x, table_y, table_z):
    highest = lax.Precision.HIGHEST
    spectral = jnp.einsum("ia,abc->ibc", table_x, values, precision=highest)
    spectral = jnp.einsum("jb,ibc->ijc", table_y, spectral, precision=highest)
    return jnp.einsum("kc,ijc->ijk", table_z, spectral, precision=highest)


def coarse_solve(source, factor):
    size_x, size_y, size_z = source.shape
    table_x = sine_table(size_x)
    table_y = cosine_table(size_y)
    table_z = cosine_table(size_z)
    spectral = transform(source, table_x, table_y, table_z)
    denom = (
        sine_values(size_x)[:, None, None]
        + cosine_values(size_y)[None, :, None]
        + cosine_values(size_z)[None, None, :]
    ) * factor
    return transform(spectral / denom, table_x.T, table_y.T, table_z.T)


def mirror_edges(padded):
    low_edge = lax.axis_index("gy") == 0
    high_edge = lax.axis_index("gy") == lax.axis_size("gy") - 1
    first = jnp.where(low_edge, padded[:, 1:2], padded[:, 0:1])
    last = jnp.where(high_edge, padded[:, -2:-1], padded[:, -1:])
    return jnp.concatenate([first, padded[:, 1:-1], last], 1)


def operator_at(iterate, factor):
    padded = extended(iterate, (("gx", 0), ("gy", 1)), 1)
    return level_apply(iterate, neighbours(mirror_edges(padded)), factor)


def assemble(pieces, cells_x, cells_y, cells_z):
    count_x = lax.axis_size("gx")
    count_y = lax.axis_size("gy")
    return (
        pieces.reshape(count_x, count_y, cells_x, cells_y, cells_z)
        .transpose(0, 2, 1, 3, 4)
        .reshape(count_x * cells_x, count_y * cells_y, cells_z)
    )


def own_tile(whole, cells_x, cells_y, cells_z):
    start_x = lax.axis_index("gx") * cells_x
    start_y = lax.axis_index("gy") * cells_y
    return lax.dynamic_slice(
        whole, (start_x, start_y, jnp.zeros((), jnp.int32)), (cells_x, cells_y, cells_z)
    )


def coarse_part(source, factor):
    cells_x, cells_y, cells_z = source.shape
    pieces = lax.all_gather(source[None], ("gx", "gy"), axis=0, tiled=True)
    entire = assemble(pieces, cells_x, cells_y, cells_z)
    solved = coarse_solve(entire, factor)
    return own_tile(solved, cells_x, cells_y, cells_z)


def body(state, pinning, lead_values):
    padded = extended(state, (("gx", 1), ("gy", 2)), 1)
    padded = jnp.pad(padded, ((0, 0), (0, 0), (0, 0), (1, 1)))
    rate_re, rate_im, rates_link, divergence, here_re, here_im = flow_terms(padded, pinning)
    cells_x = state.shape[1]
    global_x = lax.axis_index("gx") * cells_x + jnp.arange(cells_x)
    last_x = cells_x * lax.axis_size("gx") - 1
    lead_term = jnp.where((global_x == 0)[:, None, None], lead_values[0][None], 0.0) + jnp.where(
        (global_x == last_x)[:, None, None], lead_values[1][None], 0.0
    )
    tiled_levels = LEVELS - 1
    sources = [lead_term - divergence]
    saved = []
    for layer_no in range(tiled_levels):
        factor = 0.25**layer_no
        source = sources[layer_no]
        blank = jnp.zeros_like(source)
        iterate = jacobi_sweep(blank, blank, source, factor)
        for sweep_no in range(PRE - 1):
            iterate = jacobi_sweep(iterate, operator_at(iterate, factor), source, factor)
        saved.append(iterate)
        sources.append(restrict(source - operator_at(iterate, factor)))
    low_source = sources[tiled_levels]
    iterate = coarse_part(low_source, 0.25 ** (LEVELS - 1))
    for layer_no in reversed(range(tiled_levels)):
        factor = 0.25**layer_no
        iterate = saved[layer_no] + prolong(iterate)
        for sweep_no in range(POST):
            iterate = jacobi_sweep(iterate, operator_at(iterate, factor), sources[layer_no], factor)
    after_x = shifted(iterate[:1], "gx", -1)
    after_y = shifted(iterate[:, :1], "gy", -1)
    grad_x = jnp.concatenate([iterate[1:], after_x], 0) - iterate
    grad_y = jnp.concatenate([iterate[:, 1:], after_y], 1) - iterate
    grad_z = jnp.concatenate([iterate[:, :, 1:], jnp.zeros_like(iterate[:, :, :1])], 2) - iterate
    final_re = rate_re + iterate * here_im
    final_im = rate_im - iterate * here_re
    rates = jnp.stack(
        [final_re, final_im, rates_link[0] - grad_x, rates_link[1] - grad_y, rates_link[2] - grad_z]
    )
    return (state + DT * rates, iterate)


def solution(mesh):
    placed = (P(None, "gx", "gy", None), P("gx", "gy", None), P(None, "gy", None))
    return jax.shard_map(
        body,
        mesh=mesh,
        in_specs=placed,
        out_specs=(P(None, "gx", "gy", None), P("gx", "gy", None)),
        check_vma=False,
    )
```

profile of v0, /device:TPU:100, one launch (start us, length us, event | category | flops | bytes accessed | tf_op | source)
XLA Modules:
  0.0 463.0 jit_solution(6861424637704271208)
XLA Ops:
  3.3 5.8 %collective-permute-start.1 = (f32[5,1,8,128]{3,2,1,0:T(8,128)S(1)}, f32[5,1,8,128]{3,2,1,0:T(8,128)S(1)}, u32[]{:S(2)}, u32[]{:S(2)}) collective-permute-start(f32[5,1,8,128]{3,2,1,0:T(8,128)S(1)} %get-tuple-element.39), channel_id=1, source_target_pairs={{16,0},{32,16},{48,32},{64,48},{80,64},{96,80},{112,96},{128,112},... | collective-permute-start | bytes 61448 | tf_op jit(solution)/shard_map/ppermute | solution.py:28
  10.9 5.0 %collective-permute-start.2 = (f32[5,18,1,128]{3,2,1,0:T(1,128)S(1)}, f32[5,18,1,128]{3,2,1,0:T(1,128)S(1)}, u32[]{:S(2)}, u32[]{:S(2)}) collective-permute-start(f32[5,18,1,128]{3,2,1,0:T(1,128)S(1)} %get-tuple-element.37), channel_id=1, source_target_pairs={{0,1},{1,2},{2,3},{3,4},{4,5},{5,6},{6,7},{7,8},{8,9},{9,10},{10,1... | collective-permute-start | bytes 138248 | tf_op jit(solution)/shard_map/ppermute | solution.py:26
  15.9 1.9 collective-permute-start.3
  17.9 5.2 %collective-permute-done.3 = f32[5,18,1,128]{3,2,1,0:T(1,128)S(1)} collective-permute-done((f32[5,18,1,128]{3,2,1,0:T(1,128)S(1)}, f32[5,18,1,128]{3,2,1,0:T(1,128)S(1)}, u32[]{:S(2)}, u32[]{:S(2)}) %collective-permute-start.3) | collective-permute-done | bytes 46112 | tf_op jit(solution)/shard_map/ppermute | solution.py:28
  25.9 4.0 collective-permute-start.4
  31.9 5.1 %collective-permute-done.5 = f32[1,8,128]{2,1,0:T(8,128)S(1)} collective-permute-done((f32[1,8,128]{2,1,0:T(8,128)S(1)}, f32[1,8,128]{2,1,0:T(8,128)S(1)}, u32[]{:S(2)}, u32[]{:S(2)}) %collective-permute-start.5) | collective-permute-done | bytes 4128 | tf_op jit(solution)/shard_map/ppermute | solution.py:26
  38.9 5.1 %collective-permute-start.7 = (f32[18,1,128]{2,1,0:T(1,128)S(1)}, f32[18,1,128]{2,1,0:T(1,128)S(1)}, u32[]{:S(2)}, u32[]{:S(2)}) collective-permute-start(f32[18,1,128]{2,1,0:T(1,128)S(1)} %get-tuple-element.80), channel_id=1, source_target_pairs={{0,1},{1,2},{2,3},{3,4},{4,5},{5,6},{6,7},{7,8},{8,9},{9,10},{10,1... | collective-permute-start | bytes 27656 | tf_op jit(solution)/shard_map/ppermute | solution.py:26
  47.7 2.4 collective-permute-start.9
  50.1 4.6 collective-permute-done.9
  56.7 5.4 %collective-permute-start.11 = (f32[18,1,128]{2,1,0:T(1,128)S(1)}, f32[18,1,128]{2,1,0:T(1,128)S(1)}, u32[]{:S(2)}, u32[]{:S(2)}) collective-permute-start(f32[18,1,128]{2,1,0:T(1,128)S(1)} %get-tuple-element.76), channel_id=1, source_target_pairs={{0,1},{1,2},{2,3},{3,4},{4,5},{5,6},{6,7},{7,8},{8,9},{9,10},{10,1... | collective-permute-start | bytes 27656 | tf_op jit(solution)/shard_map/ppermute | solution.py:26
  63.9 1.9 collective-permute-start.12
  65.8 2.4 collective-permute-start.13
  68.2 4.6 collective-permute-done.13
  74.8 5.4 %collective-permute-start.15 = (f32[18,1,128]{2,1,0:T(1,128)S(1)}, f32[18,1,128]{2,1,0:T(1,128)S(1)}, u32[]{:S(2)}, u32[]{:S(2)}) collective-permute-start(f32[18,1,128]{2,1,0:T(1,128)S(1)} %get-tuple-element.72), channel_id=1, source_target_pairs={{0,1},{1,2},{2,3},{3,4},{4,5},{5,6},{6,7},{7,8},{8,9},{9,10},{10,1... | collective-permute-start | bytes 27656 | tf_op jit(solution)/shard_map/ppermute | solution.py:26
  81.9 5.5 %reshape.145 = f32[8,2,4,2,64,2]{5,4,3,2,1,0:T(8,128)} reshape(f32[16,8,128]{2,1,0:T(8,128)S(1)} %fusion.61) | data formatting | bytes 131072 | tf_op jit(solution)/shard_map/reshape | solution.py:157
  87.5 2.5 reduce_sum.34
  90.0 1.9 collective-permute-start.16
  92.0 2.4 collective-permute-start.17
  94.4 4.6 collective-permute-done.17
  99.0 5.4 %collective-permute-start.19 = (f32[10,1,64]{2,1,0:T(1,128)S(1)}, f32[10,1,64]{2,1,0:T(1,128)S(1)}, u32[]{:S(2)}, u32[]{:S(2)}) collective-permute-start(f32[10,1,64]{2,1,0:T(1,128)S(1)} %pad_maximum_fusion.174), channel_id=1, source_target_pairs={{0,1},{1,2},{2,3},{3,4},{4,5},{5,6},{6,7},{7,8},{8,9},{9,10},{10,1... | collective-permute-start | bytes 7688 | tf_op jit(solution)/shard_map/ppermute | solution.py:26
  105.7 1.9 collective-permute-start.18
  107.7 5.1 %collective-permute-done.18 = f32[10,1,64]{2,1,0:T(1,128)S(1)} collective-permute-done((f32[10,1,64]{2,1,0:T(1,128)S(1)}, f32[10,1,64]{2,1,0:T(1,128)S(1)}, u32[]{:S(2)}, u32[]{:S(2)}) %collective-permute-start.18) | collective-permute-done | bytes 2592 | tf_op jit(solution)/shard_map/ppermute | solution.py:28
  113.0 1.9 collective-permute-start.20
  114.9 2.4 collective-permute-start.21
  117.3 4.6 collective-permute-done.21
  121.9 3.9 collective-permute-start.23
  129.4 4.8 %collective-permute-done.22 = f32[10,1,64]{2,1,0:T(1,128)S(1)} collective-permute-done((f32[10,1,64]{2,1,0:T(1,128)S(1)}, f32[10,1,64]{2,1,0:T(1,128)S(1)}, u32[]{:S(2)}, u32[]{:S(2)}) %collective-permute-start.22) | collective-permute-done | bytes 2592 | tf_op jit(solution)/shard_map/ppermute | solution.py:28
  136.4 2.4 collective-permute-start.25
  138.8 4.6 collective-permute-done.25
  143.4 3.9 collective-permute-start.27
  148.9 1.9 collective-permute-start.26
  150.9 4.8 %collective-permute-done.26 = f32[10,1,64]{2,1,0:T(1,128)S(1)} collective-permute-done((f32[10,1,64]{2,1,0:T(1,128)S(1)}, f32[10,1,64]{2,1,0:T(1,128)S(1)}, u32[]{:S(2)}, u32[]{:S(2)}) %collective-permute-start.26) | collective-permute-done | bytes 2592 | tf_op jit(solution)/shard_map/ppermute | solution.py:28
  158.5 2.4 collective-permute-start.29
  161.0 4.6 collective-permute-done.29
  167.5 5.1 %collective-permute-start.31 = (f32[6,1,32]{2,0,1:T(8,128)S(1)}, f32[6,1,32]{2,0,1:T(8,128)S(1)}, u32[]{:S(2)}, u32[]{:S(2)}) collective-permute-start(f32[6,1,32]{2,0,1:T(8,128)S(1)} %get-tuple-element.139), channel_id=1, source_target_pairs={{0,1},{1,2},{2,3},{3,4},{4,5},{5,6},{6,7},{7,8},{8,9},{9,10},{10,1... | collective-permute-start | bytes 2312 | tf_op jit(solution)/shard_map/ppermute | solution.py:26
  176.1 2.4 collective-permute-start.33
  178.5 4.5 collective-permute-done.33
  185.0 5.4 %collective-permute-start.35 = (f32[6,1,32]{2,0,1:T(8,128)S(1)}, f32[6,1,32]{2,0,1:T(8,128)S(1)}, u32[]{:S(2)}, u32[]{:S(2)}) collective-permute-start(f32[6,1,32]{2,0,1:T(8,128)S(1)} %get-tuple-element.135), channel_id=1, source_target_pairs={{0,1},{1,2},{2,3},{3,4},{4,5},{5,6},{6,7},{7,8},{8,9},{9,10},{10,1... | collective-permute-start | bytes 2312 | tf_op jit(solution)/shard_map/ppermute | solution.py:26
  193.9 2.4 collective-permute-start.37
  196.3 4.6 collective-permute-done.37
  202.8 5.4 %collective-permute-start.39 = (f32[6,1,32]{2,0,1:T(8,128)S(1)}, f32[6,1,32]{2,0,1:T(8,128)S(1)}, u32[]{:S(2)}, u32[]{:S(2)}) collective-permute-start(f32[6,1,32]{2,0,1:T(8,128)S(1)} %get-tuple-element.131), channel_id=1, source_target_pairs={{0,1},{1,2},{2,3},{3,4},{4,5},{5,6},{6,7},{7,8},{8,9},{9,10},{10,1... | collective-permute-start | bytes 2312 | tf_op jit(solution)/shard_map/ppermute | solution.py:26
  209.9 119.3 %all-gather.1 = f32[512,2,16]{2,1,0:T(2,128)S(1)} all-gather(f32[1,2,16]{2,1,0:T(2,128)S(1)} %multiply_bitcast_fusion), channel_id=2, replica_groups=mesh['gx'=32,'gy'=16] {'gx','gy'}, dimensions={0}, use_global_device_ids=true | all-gather | bytes 65664 | tf_op jit(solution)/shard_map/all_gather | solution.py:243
  334.8 2.4 collective-permute-start.41
  337.2 4.6 collective-permute-done.41
  343.7 5.3 %collective-permute-start.43 = (f32[6,1,32]{2,0,1:T(8,128)S(1)}, f32[6,1,32]{2,0,1:T(8,128)S(1)}, u32[]{:S(2)}, u32[]{:S(2)}) collective-permute-start(f32[6,1,32]{2,0,1:T(8,128)S(1)} %get-tuple-element.127), channel_id=1, source_target_pairs={{0,1},{1,2},{2,3},{3,4},{4,5},{5,6},{6,7},{7,8},{8,9},{9,10},{10,1... | collective-permute-start | bytes 2312 | tf_op jit(solution)/shard_map/ppermute | solution.py:26
  352.3 2.4 collective-permute-start.45
  354.7 4.6 collective-permute-done.45
  359.3 2.5 collective-permute-start.46
  361.8 4.8 %collective-permute-start.47 = (f32[6,1,32]{2,0,1:T(8,128)S(1)}, f32[6,1,32]{2,0,1:T(8,128)S(1)}, u32[]{:S(2)}, u32[]{:S(2)}) collective-permute-start(f32[6,1,32]{2,0,1:T(8,128)S(1)} %get-tuple-element.123), channel_id=1, source_target_pairs={{0,1},{1,2},{2,3},{3,4},{4,5},{5,6},{6,7},{7,8},{8,9},{9,10},{10,1... | collective-permute-start | bytes 2312 | tf_op jit(solution)/shard_map/ppermute | solution.py:26
  370.3 2.4 collective-permute-start.49
  372.8 4.6 collective-permute-done.49
  377.4 5.4 %collective-permute-start.51 = (f32[10,1,64]{2,1,0:T(1,128)S(1)}, f32[10,1,64]{2,1,0:T(1,128)S(1)}, u32[]{:S(2)}, u32[]{:S(2)}) collective-permute-start(f32[10,1,64]{2,1,0:T(1,128)S(1)} %pad_maximum_fusion.165), channel_id=1, source_target_pairs={{0,1},{1,2},{2,3},{3,4},{4,5},{5,6},{6,7},{7,8},{8,9},{9,10},{10,1... | collective-permute-start | bytes 7688 | tf_op jit(solution)/shard_map/ppermute | solution.py:26
  386.0 5.1 %collective-permute-done.50 = f32[10,1,64]{2,1,0:T(1,128)S(1)} collective-permute-done((f32[10,1,64]{2,1,0:T(1,128)S(1)}, f32[10,1,64]{2,1,0:T(1,128)S(1)}, u32[]{:S(2)}, u32[]{:S(2)}) %collective-permute-start.50) | collective-permute-done | bytes 2592 | tf_op jit(solution)/shard_map/ppermute | solution.py:28
  393.3 2.4 collective-permute-start.53
  395.7 4.6 collective-permute-done.53
  400.3 3.9 collective-permute-start.55
  407.8 4.8 %collective-permute-done.54 = f32[10,1,64]{2,1,0:T(1,128)S(1)} collective-permute-done((f32[10,1,64]{2,1,0:T(1,128)S(1)}, f32[10,1,64]{2,1,0:T(1,128)S(1)}, u32[]{:S(2)}, u32[]{:S(2)}) %collective-permute-start.54) | collective-permute-done | bytes 2592 | tf_op jit(solution)/shard_map/ppermute | solution.py:28
  415.3 2.4 collective-permute-start.57
  417.7 4.6 collective-permute-done.57
  424.3 5.1 %collective-permute-start.59 = (f32[18,1,128]{2,1,0:T(1,128)S(1)}, f32[18,1,128]{2,1,0:T(1,128)S(1)}, u32[]{:S(2)}, u32[]{:S(2)}) collective-permute-start(f32[18,1,128]{2,1,0:T(1,128)S(1)} %get-tuple-element.68), channel_id=1, source_target_pairs={{0,1},{1,2},{2,3},{3,4},{4,5},{5,6},{6,7},{7,8},{8,9},{9,10},{10,1... | collective-permute-start | bytes 27656 | tf_op jit(solution)/shard_map/ppermute | solution.py:26
  433.1 2.4 collective-permute-start.61
  435.5 4.6 collective-permute-done.61
  442.1 5.4 %collective-permute-start.63 = (f32[18,1,128]{2,1,0:T(1,128)S(1)}, f32[18,1,128]{2,1,0:T(1,128)S(1)}, u32[]{:S(2)}, u32[]{:S(2)}) collective-permute-start(f32[18,1,128]{2,1,0:T(1,128)S(1)} %get-tuple-element.64), channel_id=1, source_target_pairs={{0,1},{1,2},{2,3},{3,4},{4,5},{5,6},{6,7},{7,8},{8,9},{9,10},{10,1... | collective-permute-start | bytes 27656 | tf_op jit(solution)/shard_map/ppermute | solution.py:26
  457.0 4.8 %collective-permute-done.65 = f32[16,1,128]{2,1,0:T(1,128)S(1)} collective-permute-done((f32[16,1,128]{2,1,0:T(1,128)S(1)}, f32[16,1,128]{2,1,0:T(1,128)S(1)}, u32[]{:S(2)}, u32[]{:S(2)}) %collective-permute-start.65) | collective-permute-done | bytes 8224 | tf_op jit(solution)/shard_map/ppermute | solution.py:38
  (258 shorter events, 92.0 us)
Async XLA Ops:
  1.4 8.4 %collective-permute-start = (f32[5,1,8,128]{3,2,1,0:T(8,128)S(1)}, f32[5,1,8,128]{3,2,1,0:T(8,128)S(1)}, u32[]{:S(2)}, u32[]{:S(2)}) collective-permute-start(f32[5,1,8,128]{3,2,1,0:T(8,128)S(1)} %get-tuple-element.40), channel_id=1, source_target_pairs={{0,16},{16,32},{32,48},{48,64},{64,80},{80,96},{96,112},{112,128},... | collective-permute-start | bytes 61448 | tf_op jit(solution)/shard_map/ppermute | solution.py:26
  3.3 7.5 %collective-permute-start.1 = (f32[5,1,8,128]{3,2,1,0:T(8,128)S(1)}, f32[5,1,8,128]{3,2,1,0:T(8,128)S(1)}, u32[]{:S(2)}, u32[]{:S(2)}) collective-permute-start(f32[5,1,8,128]{3,2,1,0:T(8,128)S(1)} %get-tuple-element.39), channel_id=1, source_target_pairs={{16,0},{32,16},{48,32},{64,48},{80,64},{96,80},{112,96},{128,112},... | collective-permute-start | bytes 61448 | tf_op jit(solution)/shard_map/ppermute | solution.py:28
  10.9 7.0 %collective-permute-start.2 = (f32[5,18,1,128]{3,2,1,0:T(1,128)S(1)}, f32[5,18,1,128]{3,2,1,0:T(1,128)S(1)}, u32[]{:S(2)}, u32[]{:S(2)}) collective-permute-start(f32[5,18,1,128]{3,2,1,0:T(1,128)S(1)} %get-tuple-element.37), channel_id=1, source_target_pairs={{0,1},{1,2},{2,3},{3,4},{4,5},{5,6},{6,7},{7,8},{8,9},{9,10},{10,1... | collective-permute-start | bytes 138248 | tf_op jit(solution)/shard_map/ppermute | solution.py:26
  15.9 7.2 %collective-permute-start.3 = (f32[5,18,1,128]{3,2,1,0:T(1,128)S(1)}, f32[5,18,1,128]{3,2,1,0:T(1,128)S(1)}, u32[]{:S(2)}, u32[]{:S(2)}) collective-permute-start(f32[5,18,1,128]{3,2,1,0:T(1,128)S(1)} %get-tuple-element.38), channel_id=1, source_target_pairs={{1,0},{2,1},{3,2},{4,3},{5,4},{6,5},{7,6},{8,7},{9,8},{10,9},{11,1... | collective-permute-start | bytes 138248 | tf_op jit(solution)/shard_map/ppermute | solution.py:28
  25.9 6.0 %collective-permute-start.4 = (f32[1,8,128]{2,1,0:T(8,128)S(1)}, f32[1,8,128]{2,1,0:T(8,128)S(1)}, u32[]{:S(2)}, u32[]{:S(2)}) collective-permute-start(f32[1,8,128]{2,1,0:T(8,128)S(1)} %get-tuple-element.90), channel_id=1, source_target_pairs={{16,0},{32,16},{48,32},{64,48},{80,64},{96,80},{112,96},{128,112},... | collective-permute-start | bytes 12296 | tf_op jit(solution)/shard_map/ppermute | solution.py:28
  29.9 7.0 %collective-permute-start.5 = (f32[1,8,128]{2,1,0:T(8,128)S(1)}, f32[1,8,128]{2,1,0:T(8,128)S(1)}, u32[]{:S(2)}, u32[]{:S(2)}) collective-permute-start(f32[1,8,128]{2,1,0:T(8,128)S(1)} %get-tuple-element.89), channel_id=1, source_target_pairs={{0,16},{16,32},{32,48},{48,64},{64,80},{80,96},{96,112},{112,128},... | collective-permute-start | bytes 12296 | tf_op jit(solution)/shard_map/ppermute | solution.py:26
  37.0 7.1 %collective-permute-start.6 = (f32[18,1,128]{2,1,0:T(1,128)S(1)}, f32[18,1,128]{2,1,0:T(1,128)S(1)}, u32[]{:S(2)}, u32[]{:S(2)}) collective-permute-start(f32[18,1,128]{2,1,0:T(1,128)S(1)} %get-tuple-element.79), channel_id=1, source_target_pairs={{1,0},{2,1},{3,2},{4,3},{5,4},{6,5},{7,6},{8,7},{9,8},{10,9},{11,1... | collective-permute-start | bytes 27656 | tf_op jit(solution)/shard_map/ppermute | solution.py:28
  38.9 6.5 %collective-permute-start.7 = (f32[18,1,128]{2,1,0:T(1,128)S(1)}, f32[18,1,128]{2,1,0:T(1,128)S(1)}, u32[]{:S(2)}, u32[]{:S(2)}) collective-permute-start(f32[18,1,128]{2,1,0:T(1,128)S(1)} %get-tuple-element.80), channel_id=1, source_target_pairs={{0,1},{1,2},{2,3},{3,4},{4,5},{5,6},{6,7},{7,8},{8,9},{9,10},{10,1... | collective-permute-start | bytes 27656 | tf_op jit(solution)/shard_map/ppermute | solution.py:26
  45.8 4.3 collective-permute-start.8
  47.7 7.0 %collective-permute-start.9 = (f32[1,8,128]{2,1,0:T(8,128)S(1)}, f32[1,8,128]{2,1,0:T(8,128)S(1)}, u32[]{:S(2)}, u32[]{:S(2)}) collective-permute-start(f32[1,8,128]{2,1,0:T(8,128)S(1)} %get-tuple-element.87), channel_id=1, source_target_pairs={{0,16},{16,32},{32,48},{48,64},{64,80},{80,96},{96,112},{112,128},... | collective-permute-start | bytes 12296 | tf_op jit(solution)/shard_map/ppermute | solution.py:26
  54.8 7.3 %collective-permute-start.10 = (f32[18,1,128]{2,1,0:T(1,128)S(1)}, f32[18,1,128]{2,1,0:T(1,128)S(1)}, u32[]{:S(2)}, u32[]{:S(2)}) collective-permute-start(f32[18,1,128]{2,1,0:T(1,128)S(1)} %get-tuple-element.75), channel_id=1, source_target_pairs={{1,0},{2,1},{3,2},{4,3},{5,4},{6,5},{7,6},{8,7},{9,8},{10,9},{11,1... | collective-permute-start | bytes 27656 | tf_op jit(solution)/shard_map/ppermute | solution.py:28
  56.7 6.8 %collective-permute-start.11 = (f32[18,1,128]{2,1,0:T(1,128)S(1)}, f32[18,1,128]{2,1,0:T(1,128)S(1)}, u32[]{:S(2)}, u32[]{:S(2)}) collective-permute-start(f32[18,1,128]{2,1,0:T(1,128)S(1)} %get-tuple-element.76), channel_id=1, source_target_pairs={{0,1},{1,2},{2,3},{3,4},{4,5},{5,6},{6,7},{7,8},{8,9},{9,10},{10,1... | collective-permute-start | bytes 27656 | tf_op jit(solution)/shard_map/ppermute | solution.py:26
  63.9 4.3 collective-permute-start.12
  65.8 7.0 %collective-permute-start.13 = (f32[1,8,128]{2,1,0:T(8,128)S(1)}, f32[1,8,128]{2,1,0:T(8,128)S(1)}, u32[]{:S(2)}, u32[]{:S(2)}) collective-permute-start(f32[1,8,128]{2,1,0:T(8,128)S(1)} %get-tuple-element.85), channel_id=1, source_target_pairs={{0,16},{16,32},{32,48},{48,64},{64,80},{80,96},{96,112},{112,128},... | collective-permute-start | bytes 12296 | tf_op jit(solution)/shard_map/ppermute | solution.py:26
  72.9 7.3 %collective-permute-start.14 = (f32[18,1,128]{2,1,0:T(1,128)S(1)}, f32[18,1,128]{2,1,0:T(1,128)S(1)}, u32[]{:S(2)}, u32[]{:S(2)}) collective-permute-start(f32[18,1,128]{2,1,0:T(1,128)S(1)} %get-tuple-element.71), channel_id=1, source_target_pairs={{1,0},{2,1},{3,2},{4,3},{5,4},{6,5},{7,6},{8,7},{9,8},{10,9},{11,1... | collective-permute-start | bytes 27656 | tf_op jit(solution)/shard_map/ppermute | solution.py:28
  74.8 6.8 %collective-permute-start.15 = (f32[18,1,128]{2,1,0:T(1,128)S(1)}, f32[18,1,128]{2,1,0:T(1,128)S(1)}, u32[]{:S(2)}, u32[]{:S(2)}) collective-permute-start(f32[18,1,128]{2,1,0:T(1,128)S(1)} %get-tuple-element.72), channel_id=1, source_target_pairs={{0,1},{1,2},{2,3},{3,4},{4,5},{5,6},{6,7},{7,8},{8,9},{9,10},{10,1... | collective-permute-start | bytes 27656 | tf_op jit(solution)/shard_map/ppermute | solution.py:26
  90.0 4.3 collective-permute-start.16
  92.0 7.0 %collective-permute-start.17 = (f32[1,4,64]{2,1,0:T(4,128)S(1)}, f32[1,4,64]{2,1,0:T(4,128)S(1)}, u32[]{:S(2)}, u32[]{:S(2)}) collective-permute-start(f32[1,4,64]{2,1,0:T(4,128)S(1)} %get-tuple-element.119), channel_id=1, source_target_pairs={{0,16},{16,32},{32,48},{48,64},{64,80},{80,96},{96,112},{112,128},... | collective-permute-start | bytes 3080 | tf_op jit(solution)/shard_map/ppermute | solution.py:26
  99.0 6.7 %collective-permute-start.19 = (f32[10,1,64]{2,1,0:T(1,128)S(1)}, f32[10,1,64]{2,1,0:T(1,128)S(1)}, u32[]{:S(2)}, u32[]{:S(2)}) collective-permute-start(f32[10,1,64]{2,1,0:T(1,128)S(1)} %pad_maximum_fusion.174), channel_id=1, source_target_pairs={{0,1},{1,2},{2,3},{3,4},{4,5},{5,6},{6,7},{7,8},{8,9},{9,10},{10,1... | collective-permute-start | bytes 7688 | tf_op jit(solution)/shard_map/ppermute | solution.py:26
  105.7 7.0 %collective-permute-start.18 = (f32[10,1,64]{2,1,0:T(1,128)S(1)}, f32[10,1,64]{2,1,0:T(1,128)S(1)}, u32[]{:S(2)}, u32[]{:S(2)}) collective-permute-start(f32[10,1,64]{2,1,0:T(1,128)S(1)} %get-tuple-element.26), channel_id=1, source_target_pairs={{1,0},{2,1},{3,2},{4,3},{5,4},{6,5},{7,6},{8,7},{9,8},{10,9},{11,1... | collective-permute-start | bytes 7688 | tf_op jit(solution)/shard_map/ppermute | solution.py:28
  113.0 4.3 collective-permute-start.20
  114.9 7.0 %collective-permute-start.21 = (f32[1,4,64]{2,1,0:T(4,128)S(1)}, f32[1,4,64]{2,1,0:T(4,128)S(1)}, u32[]{:S(2)}, u32[]{:S(2)}) collective-permute-start(f32[1,4,64]{2,1,0:T(4,128)S(1)} %get-tuple-element.117), channel_id=1, source_target_pairs={{0,16},{16,32},{32,48},{48,64},{64,80},{80,96},{96,112},{112,128},... | collective-permute-start | bytes 3080 | tf_op jit(solution)/shard_map/ppermute | solution.py:26
  121.9 5.5 %collective-permute-start.23 = (f32[10,1,64]{2,1,0:T(1,128)S(1)}, f32[10,1,64]{2,1,0:T(1,128)S(1)}, u32[]{:S(2)}, u32[]{:S(2)}) collective-permute-start(f32[10,1,64]{2,1,0:T(1,128)S(1)} %pad_maximum_fusion.171), channel_id=1, source_target_pairs={{0,1},{1,2},{2,3},{3,4},{4,5},{5,6},{6,7},{7,8},{8,9},{9,10},{10,1... | collective-permute-start | bytes 7688 | tf_op jit(solution)/shard_map/ppermute | solution.py:26
  127.5 6.7 %collective-permute-start.22 = (f32[10,1,64]{2,1,0:T(1,128)S(1)}, f32[10,1,64]{2,1,0:T(1,128)S(1)}, u32[]{:S(2)}, u32[]{:S(2)}) collective-permute-start(f32[10,1,64]{2,1,0:T(1,128)S(1)} %get-tuple-element.24), channel_id=1, source_target_pairs={{1,0},{2,1},{3,2},{4,3},{5,4},{6,5},{7,6},{8,7},{9,8},{10,9},{11,1... | collective-permute-start | bytes 7688 | tf_op jit(solution)/shard_map/ppermute | solution.py:28
  134.5 4.3 collective-permute-start.24
  136.4 7.0 %collective-permute-start.25 = (f32[1,4,64]{2,1,0:T(4,128)S(1)}, f32[1,4,64]{2,1,0:T(4,128)S(1)}, u32[]{:S(2)}, u32[]{:S(2)}) collective-permute-start(f32[1,4,64]{2,1,0:T(4,128)S(1)} %get-tuple-element.115), channel_id=1, source_target_pairs={{0,16},{16,32},{32,48},{48,64},{64,80},{80,96},{96,112},{112,128},... | collective-permute-start | bytes 3080 | tf_op jit(solution)/shard_map/ppermute | solution.py:26
  143.4 5.5 %collective-permute-start.27 = (f32[10,1,64]{2,1,0:T(1,128)S(1)}, f32[10,1,64]{2,1,0:T(1,128)S(1)}, u32[]{:S(2)}, u32[]{:S(2)}) collective-permute-start(f32[10,1,64]{2,1,0:T(1,128)S(1)} %pad_maximum_fusion.168), channel_id=1, source_target_pairs={{0,1},{1,2},{2,3},{3,4},{4,5},{5,6},{6,7},{7,8},{8,9},{9,10},{10,1... | collective-permute-start | bytes 7688 | tf_op jit(solution)/shard_map/ppermute | solution.py:26
  148.9 6.7 %collective-permute-start.26 = (f32[10,1,64]{2,1,0:T(1,128)S(1)}, f32[10,1,64]{2,1,0:T(1,128)S(1)}, u32[]{:S(2)}, u32[]{:S(2)}) collective-permute-start(f32[10,1,64]{2,1,0:T(1,128)S(1)} %get-tuple-element.22), channel_id=1, source_target_pairs={{1,0},{2,1},{3,2},{4,3},{5,4},{6,5},{7,6},{8,7},{9,8},{10,9},{11,1... | collective-permute-start | bytes 7688 | tf_op jit(solution)/shard_map/ppermute | solution.py:28
  156.6 4.3 collective-permute-start.28
  158.5 7.0 %collective-permute-start.29 = (f32[1,2,32]{2,0,1:T(1,128)S(1)}, f32[1,2,32]{2,0,1:T(1,128)S(1)}, u32[]{:S(2)}, u32[]{:S(2)}) collective-permute-start(f32[1,2,32]{2,0,1:T(1,128)S(1)} %get-tuple-element.151), channel_id=1, source_target_pairs={{0,16},{16,32},{32,48},{48,64},{64,80},{80,96},{96,112},{112,128},... | collective-permute-start | bytes 776 | tf_op jit(solution)/shard_map/ppermute | solution.py:26
  165.6 7.1 %collective-permute-start.30 = (f32[6,1,32]{2,0,1:T(8,128)S(1)}, f32[6,1,32]{2,0,1:T(8,128)S(1)}, u32[]{:S(2)}, u32[]{:S(2)}) collective-permute-start(f32[6,1,32]{2,0,1:T(8,128)S(1)} %get-tuple-element.140), channel_id=1, source_target_pairs={{1,0},{2,1},{3,2},{4,3},{5,4},{6,5},{7,6},{8,7},{9,8},{10,9},{11,1... | collective-permute-start | bytes 2312 | tf_op jit(solution)/shard_map/ppermute | solution.py:28
  167.5 6.4 %collective-permute-start.31 = (f32[6,1,32]{2,0,1:T(8,128)S(1)}, f32[6,1,32]{2,0,1:T(8,128)S(1)}, u32[]{:S(2)}, u32[]{:S(2)}) collective-permute-start(f32[6,1,32]{2,0,1:T(8,128)S(1)} %get-tuple-element.139), channel_id=1, source_target_pairs={{0,1},{1,2},{2,3},{3,4},{4,5},{5,6},{6,7},{7,8},{8,9},{9,10},{10,1... | collective-permute-start | bytes 2312 | tf_op jit(solution)/shard_map/ppermute | solution.py:26
  174.1 4.4 collective-permute-start.32
  176.1 7.0 %collective-permute-start.33 = (f32[1,2,32]{2,0,1:T(1,128)S(1)}, f32[1,2,32]{2,0,1:T(1,128)S(1)}, u32[]{:S(2)}, u32[]{:S(2)}) collective-permute-start(f32[1,2,32]{2,0,1:T(1,128)S(1)} %get-tuple-element.149), channel_id=1, source_target_pairs={{0,16},{16,32},{32,48},{48,64},{64,80},{80,96},{96,112},{112,128},... | collective-permute-start | bytes 776 | tf_op jit(solution)/shard_map/ppermute | solution.py:26
  183.1 7.4 %collective-permute-start.34 = (f32[6,1,32]{2,0,1:T(8,128)S(1)}, f32[6,1,32]{2,0,1:T(8,128)S(1)}, u32[]{:S(2)}, u32[]{:S(2)}) collective-permute-start(f32[6,1,32]{2,0,1:T(8,128)S(1)} %get-tuple-element.136), channel_id=1, source_target_pairs={{1,0},{2,1},{3,2},{4,3},{5,4},{6,5},{7,6},{8,7},{9,8},{10,9},{11,1... | collective-permute-start | bytes 2312 | tf_op jit(solution)/shard_map/ppermute | solution.py:28
  185.0 6.7 %collective-permute-start.35 = (f32[6,1,32]{2,0,1:T(8,128)S(1)}, f32[6,1,32]{2,0,1:T(8,128)S(1)}, u32[]{:S(2)}, u32[]{:S(2)}) collective-permute-start(f32[6,1,32]{2,0,1:T(8,128)S(1)} %get-tuple-element.135), channel_id=1, source_target_pairs={{0,1},{1,2},{2,3},{3,4},{4,5},{5,6},{6,7},{7,8},{8,9},{9,10},{10,1... | collective-permute-start | bytes 2312 | tf_op jit(solution)/shard_map/ppermute | solution.py:26
  191.9 4.4 collective-permute-start.36
  193.9 7.0 %collective-permute-start.37 = (f32[1,2,32]{2,0,1:T(1,128)S(1)}, f32[1,2,32]{2,0,1:T(1,128)S(1)}, u32[]{:S(2)}, u32[]{:S(2)}) collective-permute-start(f32[1,2,32]{2,0,1:T(1,128)S(1)} %get-tuple-element.147), channel_id=1, source_target_pairs={{0,16},{16,32},{32,48},{48,64},{64,80},{80,96},{96,112},{112,128},... | collective-permute-start | bytes 776 | tf_op jit(solution)/shard_map/ppermute | solution.py:26
  200.9 7.4 %collective-permute-start.38 = (f32[6,1,32]{2,0,1:T(8,128)S(1)}, f32[6,1,32]{2,0,1:T(8,128)S(1)}, u32[]{:S(2)}, u32[]{:S(2)}) collective-permute-start(f32[6,1,32]{2,0,1:T(8,128)S(1)} %get-tuple-element.132), channel_id=1, source_target_pairs={{1,0},{2,1},{3,2},{4,3},{5,4},{6,5},{7,6},{8,7},{9,8},{10,9},{11,1... | collective-permute-start | bytes 2312 | tf_op jit(solution)/shard_map/ppermute | solution.py:28
  202.8 6.7 %collective-permute-start.39 = (f32[6,1,32]{2,0,1:T(8,128)S(1)}, f32[6,1,32]{2,0,1:T(8,128)S(1)}, u32[]{:S(2)}, u32[]{:S(2)}) collective-permute-start(f32[6,1,32]{2,0,1:T(8,128)S(1)} %get-tuple-element.131), channel_id=1, source_target_pairs={{0,1},{1,2},{2,3},{3,4},{4,5},{5,6},{6,7},{7,8},{8,9},{9,10},{10,1... | collective-permute-start | bytes 2312 | tf_op jit(solution)/shard_map/ppermute | solution.py:26
  334.8 7.0 %collective-permute-start.41 = (f32[1,2,32]{2,0,1:T(1,128)S(1)}, f32[1,2,32]{2,0,1:T(1,128)S(1)}, u32[]{:S(2)}, u32[]{:S(2)}) collective-permute-start(f32[1,2,32]{2,0,1:T(1,128)S(1)} %get-tuple-element.145), channel_id=1, source_target_pairs={{0,16},{16,32},{32,48},{48,64},{64,80},{80,96},{96,112},{112,128},... | collective-permute-start | bytes 776 | tf_op jit(solution)/shard_map/ppermute | solution.py:26
  341.8 7.3 %collective-permute-start.42 = (f32[6,1,32]{2,0,1:T(8,128)S(1)}, f32[6,1,32]{2,0,1:T(8,128)S(1)}, u32[]{:S(2)}, u32[]{:S(2)}) collective-permute-start(f32[6,1,32]{2,0,1:T(8,128)S(1)} %get-tuple-element.128), channel_id=1, source_target_pairs={{1,0},{2,1},{3,2},{4,3},{5,4},{6,5},{7,6},{8,7},{9,8},{10,9},{11,1... | collective-permute-start | bytes 2312 | tf_op jit(solution)/shard_map/ppermute | solution.py:28
  343.7 6.4 %collective-permute-start.43 = (f32[6,1,32]{2,0,1:T(8,128)S(1)}, f32[6,1,32]{2,0,1:T(8,128)S(1)}, u32[]{:S(2)}, u32[]{:S(2)}) collective-permute-start(f32[6,1,32]{2,0,1:T(8,128)S(1)} %get-tuple-element.127), channel_id=1, source_target_pairs={{0,1},{1,2},{2,3},{3,4},{4,5},{5,6},{6,7},{7,8},{8,9},{9,10},{10,1... | collective-permute-start | bytes 2312 | tf_op jit(solution)/shard_map/ppermute | solution.py:26
  350.4 4.3 collective-permute-start.44
  352.3 7.0 %collective-permute-start.45 = (f32[1,2,32]{2,0,1:T(1,128)S(1)}, f32[1,2,32]{2,0,1:T(1,128)S(1)}, u32[]{:S(2)}, u32[]{:S(2)}) collective-permute-start(f32[1,2,32]{2,0,1:T(1,128)S(1)} %get-tuple-element.143), channel_id=1, source_target_pairs={{0,16},{16,32},{32,48},{48,64},{64,80},{80,96},{96,112},{112,128},... | collective-permute-start | bytes 776 | tf_op jit(solution)/shard_map/ppermute | solution.py:26
  359.3 7.3 %collective-permute-start.46 = (f32[6,1,32]{2,0,1:T(8,128)S(1)}, f32[6,1,32]{2,0,1:T(8,128)S(1)}, u32[]{:S(2)}, u32[]{:S(2)}) collective-permute-start(f32[6,1,32]{2,0,1:T(8,128)S(1)} %get-tuple-element.124), channel_id=1, source_target_pairs={{1,0},{2,1},{3,2},{4,3},{5,4},{6,5},{7,6},{8,7},{9,8},{10,9},{11,1... | collective-permute-start | bytes 2312 | tf_op jit(solution)/shard_map/ppermute | solution.py:28
  361.8 6.2 %collective-permute-start.47 = (f32[6,1,32]{2,0,1:T(8,128)S(1)}, f32[6,1,32]{2,0,1:T(8,128)S(1)}, u32[]{:S(2)}, u32[]{:S(2)}) collective-permute-start(f32[6,1,32]{2,0,1:T(8,128)S(1)} %get-tuple-element.123), channel_id=1, source_target_pairs={{0,1},{1,2},{2,3},{3,4},{4,5},{5,6},{6,7},{7,8},{8,9},{9,10},{10,1... | collective-permute-start | bytes 2312 | tf_op jit(solution)/shard_map/ppermute | solution.py:26
  368.4 4.3 collective-permute-start.48
  370.3 7.0 %collective-permute-start.49 = (f32[1,4,64]{2,1,0:T(4,128)S(1)}, f32[1,4,64]{2,1,0:T(4,128)S(1)}, u32[]{:S(2)}, u32[]{:S(2)}) collective-permute-start(f32[1,4,64]{2,1,0:T(4,128)S(1)} %get-tuple-element.103), channel_id=1, source_target_pairs={{0,16},{16,32},{32,48},{48,64},{64,80},{80,96},{96,112},{112,128},... | collective-permute-start | bytes 3080 | tf_op jit(solution)/shard_map/ppermute | solution.py:26
  377.4 6.7 %collective-permute-start.51 = (f32[10,1,64]{2,1,0:T(1,128)S(1)}, f32[10,1,64]{2,1,0:T(1,128)S(1)}, u32[]{:S(2)}, u32[]{:S(2)}) collective-permute-start(f32[10,1,64]{2,1,0:T(1,128)S(1)} %pad_maximum_fusion.165), channel_id=1, source_target_pairs={{0,1},{1,2},{2,3},{3,4},{4,5},{5,6},{6,7},{7,8},{8,9},{9,10},{10,1... | collective-permute-start | bytes 7688 | tf_op jit(solution)/shard_map/ppermute | solution.py:26
  384.1 7.0 %collective-permute-start.50 = (f32[10,1,64]{2,1,0:T(1,128)S(1)}, f32[10,1,64]{2,1,0:T(1,128)S(1)}, u32[]{:S(2)}, u32[]{:S(2)}) collective-permute-start(f32[10,1,64]{2,1,0:T(1,128)S(1)} %get-tuple-element.20), channel_id=1, source_target_pairs={{1,0},{2,1},{3,2},{4,3},{5,4},{6,5},{7,6},{8,7},{9,8},{10,9},{11,1... | collective-permute-start | bytes 7688 | tf_op jit(solution)/shard_map/ppermute | solution.py:28
  391.4 4.3 collective-permute-start.52
  393.3 7.0 %collective-permute-start.53 = (f32[1,4,64]{2,1,0:T(4,128)S(1)}, f32[1,4,64]{2,1,0:T(4,128)S(1)}, u32[]{:S(2)}, u32[]{:S(2)}) collective-permute-start(f32[1,4,64]{2,1,0:T(4,128)S(1)} %get-tuple-element.101), channel_id=1, source_target_pairs={{0,16},{16,32},{32,48},{48,64},{64,80},{80,96},{96,112},{112,128},... | collective-permute-start | bytes 3080 | tf_op jit(solution)/shard_map/ppermute | solution.py:26
  400.3 5.5 %collective-permute-start.55 = (f32[10,1,64]{2,1,0:T(1,128)S(1)}, f32[10,1,64]{2,1,0:T(1,128)S(1)}, u32[]{:S(2)}, u32[]{:S(2)}) collective-permute-start(f32[10,1,64]{2,1,0:T(1,128)S(1)} %pad_maximum_fusion.162), channel_id=1, source_target_pairs={{0,1},{1,2},{2,3},{3,4},{4,5},{5,6},{6,7},{7,8},{8,9},{9,10},{10,1... | collective-permute-start | bytes 7688 | tf_op jit(solution)/shard_map/ppermute | solution.py:26
  405.9 6.7 %collective-permute-start.54 = (f32[10,1,64]{2,1,0:T(1,128)S(1)}, f32[10,1,64]{2,1,0:T(1,128)S(1)}, u32[]{:S(2)}, u32[]{:S(2)}) collective-permute-start(f32[10,1,64]{2,1,0:T(1,128)S(1)} %get-tuple-element.18), channel_id=1, source_target_pairs={{1,0},{2,1},{3,2},{4,3},{5,4},{6,5},{7,6},{8,7},{9,8},{10,9},{11,1... | collective-permute-start | bytes 7688 | tf_op jit(solution)/shard_map/ppermute | solution.py:28
  415.3 7.0 %collective-permute-start.57 = (f32[1,8,128]{2,1,0:T(8,128)S(1)}, f32[1,8,128]{2,1,0:T(8,128)S(1)}, u32[]{:S(2)}, u32[]{:S(2)}) collective-permute-start(f32[1,8,128]{2,1,0:T(8,128)S(1)} %get-tuple-element.83), channel_id=1, source_target_pairs={{0,16},{16,32},{32,48},{48,64},{64,80},{80,96},{96,112},{112,128},... | collective-permute-start | bytes 12296 | tf_op jit(solution)/shard_map/ppermute | solution.py:26
  422.3 7.1 %collective-permute-start.58 = (f32[18,1,128]{2,1,0:T(1,128)S(1)}, f32[18,1,128]{2,1,0:T(1,128)S(1)}, u32[]{:S(2)}, u32[]{:S(2)}) collective-permute-start(f32[18,1,128]{2,1,0:T(1,128)S(1)} %get-tuple-element.67), channel_id=1, source_target_pairs={{1,0},{2,1},{3,2},{4,3},{5,4},{6,5},{7,6},{8,7},{9,8},{10,9},{11,1... | collective-permute-start | bytes 27656 | tf_op jit(solution)/shard_map/ppermute | solution.py:28
  424.3 6.5 %collective-permute-start.59 = (f32[18,1,128]{2,1,0:T(1,128)S(1)}, f32[18,1,128]{2,1,0:T(1,128)S(1)}, u32[]{:S(2)}, u32[]{:S(2)}) collective-permute-start(f32[18,1,128]{2,1,0:T(1,128)S(1)} %get-tuple-element.68), channel_id=1, source_target_pairs={{0,1},{1,2},{2,3},{3,4},{4,5},{5,6},{6,7},{7,8},{8,9},{9,10},{10,1... | collective-permute-start | bytes 27656 | tf_op jit(solution)/shard_map/ppermute | solution.py:26
  431.2 4.3 collective-permute-start.60
  433.1 7.0 %collective-permute-start.61 = (f32[1,8,128]{2,1,0:T(8,128)S(1)}, f32[1,8,128]{2,1,0:T(8,128)S(1)}, u32[]{:S(2)}, u32[]{:S(2)}) collective-permute-start(f32[1,8,128]{2,1,0:T(8,128)S(1)} %get-tuple-element.81), channel_id=1, source_target_pairs={{0,16},{16,32},{32,48},{48,64},{64,80},{80,96},{96,112},{112,128},... | collective-permute-start | bytes 12296 | tf_op jit(solution)/shard_map/ppermute | solution.py:26
  440.2 7.3 %collective-permute-start.62 = (f32[18,1,128]{2,1,0:T(1,128)S(1)}, f32[18,1,128]{2,1,0:T(1,128)S(1)}, u32[]{:S(2)}, u32[]{:S(2)}) collective-permute-start(f32[18,1,128]{2,1,0:T(1,128)S(1)} %get-tuple-element.63), channel_id=1, source_target_pairs={{1,0},{2,1},{3,2},{4,3},{5,4},{6,5},{7,6},{8,7},{9,8},{10,9},{11,1... | collective-permute-start | bytes 27656 | tf_op jit(solution)/shard_map/ppermute | solution.py:28
  442.1 6.8 %collective-permute-start.63 = (f32[18,1,128]{2,1,0:T(1,128)S(1)}, f32[18,1,128]{2,1,0:T(1,128)S(1)}, u32[]{:S(2)}, u32[]{:S(2)}) collective-permute-start(f32[18,1,128]{2,1,0:T(1,128)S(1)} %get-tuple-element.64), channel_id=1, source_target_pairs={{0,1},{1,2},{2,3},{3,4},{4,5},{5,6},{6,7},{7,8},{8,9},{9,10},{10,1... | collective-permute-start | bytes 27656 | tf_op jit(solution)/shard_map/ppermute | solution.py:26
  451.0 5.7 %collective-permute-start.64 = (f32[1,8,128]{2,1,0:T(8,128)S(1)}, f32[1,8,128]{2,1,0:T(8,128)S(1)}, u32[]{:S(2)}, u32[]{:S(2)}) collective-permute-start(f32[1,8,128]{2,1,0:T(8,128)S(1)} %slice.1349), channel_id=1, source_target_pairs={{16,0},{32,16},{48,32},{64,48},{80,64},{96,80},{112,96},{128,112},... | collective-permute-start | bytes 12296 | tf_op jit(solution)/shard_map/ppermute | solution.py:38
  454.8 7.0 %collective-permute-start.65 = (f32[16,1,128]{2,1,0:T(1,128)S(1)}, f32[16,1,128]{2,1,0:T(1,128)S(1)}, u32[]{:S(2)}, u32[]{:S(2)}) collective-permute-start(f32[16,1,128]{2,1,0:T(1,128)S(1)} %slice.1357), channel_id=1, source_target_pairs={{1,0},{2,1},{3,2},{4,3},{5,4},{6,5},{7,6},{8,7},{9,8},{10,9},{11,1... | collective-permute-start | bytes 24584 | tf_op jit(solution)/shard_map/ppermute | solution.py:38
  (5 other events, 43.6 us)
where the time goes:
time: 465 us; the launch traced here: 463 us
  starting transfers between devices  189 us (41%)
  waiting for transfers between devices  124 us (27%)
  blocking collectives  119 us (26%)
  other arithmetic  13.2 us (3%)
  local copies, waits for them, and re-layouts  11.6 us (2%)
    all_gather x1, blocking collectives, coarse_part(): pieces = lax.all_gather(source[None], ('gx', 'gy'), axis=0, tiled=True)  119 us
    ppermute x32, starting transfers between devices, extended(): lax.ppermute(tail, axis, [(i, (i + 1) % count) for i in range(ends)])  118 us
    ppermute x32, waiting for transfers between devices, extended(): lax.ppermute(tail, axis, [(i, (i + 1) % count) for i in range(ends)])  89.5 us
    ppermute x32, starting transfers between devices, extended(): lax.ppermute(head, axis, [((i + 1) % count, i) for i in range(ends)])  68 us
    ppermute x32, waiting for transfers between devices, extended(): lax.ppermute(head, axis, [((i + 1) % count, i) for i in range(ends)])  29.8 us
  transfers between devices with their start and end apart: 66, of which 37 were waited for; matrix products, arithmetic and copies ran while one was open for 1% of the time, Pallas kernels for 0%

commit v1 on v0

v1 whole, which is shorter than its diff:
```python
import functools
import math

import jax
import jax.numpy as jnp
import ml_dtypes
import numpy as np
from jax import lax
from jax.experimental import pallas as pl
from jax.experimental.pallas import tpu as pltpu
from jax.sharding import PartitionSpec as P

MESH = pl.DeviceIdType.MESH
OMEGA = 0.8
DT = 0.05
KAPPA2 = 2.0
KEEP = 1.0 - OMEGA
GAIN = OMEGA / 6.0
TX, TY, NZ = 16, 8, 128


def chebyshev_powers(function, terms):
    fit = np.polynomial.chebyshev.Chebyshev.interpolate(
        lambda u: function(np.sqrt(np.maximum(8.0 * (u + 1.0), 0.0))), terms, domain=[-1, 1]
    )
    return [float(c) for c in np.polynomial.chebyshev.cheb2poly(fit.coef)]


COS_POWERS = chebyshev_powers(np.cos, 8)
SIN_POWERS = chebyshev_powers(lambda a: np.sinc(a / np.pi), 8)


def horner(powers, u):
    total = powers[-1] * u + powers[-2]
    for power in powers[-3::-1]:
        total = total * u + power
    return total


def cos_sin(angle):
    u = angle * angle * 0.125 - 1.0
    return horner(COS_POWERS, u), horner(SIN_POWERS, u) * angle


def sine_table(count):
    modes = np.arange(1, count + 1, dtype=np.float64)
    return np.sqrt(2.0 / (count + 1)) * np.sin(np.pi / (count + 1) * modes[:, None] * modes[None])


def sine_values(count):
    return 2.0 - 2.0 * np.cos(np.pi / (count + 1) * np.arange(1, count + 1, dtype=np.float64))


def cosine_table(count):
    modes = np.arange(count, dtype=np.float64)
    weights = np.where(modes == 0.0, 1.0, 2.0) / count
    return np.sqrt(weights)[:, None] * np.cos(
        np.pi / count * modes[:, None] * (modes[None] + 0.5)
    )


def cosine_values(count):
    return 2.0 - 2.0 * np.cos(np.pi / count * np.arange(count, dtype=np.float64))


def split_pair(table):
    high = table.astype(ml_dtypes.bfloat16)
    low = (table - high.astype(np.float64)).astype(ml_dtypes.bfloat16)
    return np.stack([high, low])


def coarse_tables(ngx, ngy):
    nx, ny, nz = 2 * ngx, ngy, 16
    groups = max(1, ngy // 8)
    width = 128 * groups
    tx, ty, tz = sine_table(nx), cosine_table(ny), cosine_table(nz)
    lanes = np.arange(128)
    along_z = np.tile(tz[:, lanes // 8].T / 8.0, (1, 8))
    along_x = np.zeros((nx, ngx, 8))
    for cell in range(8):
        place = 2 * np.arange(ngx) + cell - 3
        within = (place >= 0) & (place < nx)
        along_x[:, within, cell] = tx[:, place[within]]
    along_x = along_x.reshape(nx, ngx // 2, 2, 8).swapaxes(1, 2).reshape(nx, 8 * ngx)
    along_y = np.zeros((width, width))
    inverse = np.zeros((nx, width))
    values = (
        sine_values(nx)[:, None, None]
        + cosine_values(ny)[None, :, None]
        + cosine_values(nz)[None, None, :]
    )
    inverse[:, : ny * nz] = (1.0 / values).reshape(nx, ny * nz)
    along_y[: ny * nz, : ny * nz] = np.kron(ty.T, np.eye(nz))
    back_x = np.zeros((ngx, 16, 128))
    for cell in range(12):
        place = 2 * np.arange(ngx) + cell // 2 - 2
        within = (place >= 0) & (place < nx)
        back_x[within, cell, :nx] = tx.T[place[within]]
    back_yz = np.zeros((ny + 4, width, 128))
    for y in range(ny):
        back_yz[2 + y, : ny * nz] = np.kron(ty[:, y : y + 1], tz[:, lanes // 8])
    return (
        split_pair(along_z),
        split_pair(along_x),
        split_pair(along_y),
        inverse.astype(np.float32),
        split_pair(back_x),
        split_pair(back_yz),
    )


def halves(values):
    high = values.astype(jnp.bfloat16)
    return high, (values - high.astype(jnp.float32)).astype(jnp.bfloat16)


def product(left, right):
    dot = functools.partial(jnp.dot, preferred_element_type=jnp.float32)
    return dot(left[0], right[0]) + (dot(left[0], right[1]) + dot(left[1], right[0]))


def kernel(
    ngx,
    ngy,
    state_ref,
    pinning_ref,
    lead_ref,
    along_z_ref,
    along_x_ref,
    along_y_ref,
    inverse_ref,
    back_x_ref,
    back_yz_ref,
    out_ref,
    potential_ref,
    ext,
    pin,
    lead,
    along_z,
    along_x,
    along_y,
    inverse,
    back_x,
    back_yz,
    face_out,
    face_in,
    diag_in,
    rates,
    work,
    tile0,
    low_out,
    high_out,
    low_in,
    high_in,
    src0,
    va0,
    vb0,
    tile1,
    va1,
    vb1,
    got2,
    src2,
    va2,
    vb2,
    part0,
    pa0,
    pb0,
    part1,
    pa1,
    pb1,
    part2,
    pa2,
    pb2,
    folded,
    coarse,
    gather1,
    gather2,
    local_sem,
    state_sem,
    halo_sem,
    level0_sem,
    level1_sem,
    level2_sem,
    gather_sem,
    relay_sem,
):
    gx, gy = lax.axis_index("gx"), lax.axis_index("gy")

    def device(dx, dy):
        return (lax.rem(gx + dx % ngx, ngx), lax.rem(gy + dy % ngy, ngy))

    def each(first, last, visit):
        def one(place, carry):
            visit(place)
            return carry

        lax.fori_loop(first, last, one, 0, unroll=True)

    own_state = pltpu.make_async_copy(state_ref, ext.at[:, 1:17, 8:16], state_sem)
    own_state.start()
    barrier = pltpu.get_barrier_semaphore()
    def within(dx, dy):
        tests = [gx >= -dx] * (dx < 0) + [gx < ngx - dx] * (dx > 0)
        tests += [gy >= -dy] * (dy < 0) + [gy < ngy - dy] * (dy > 0)
        return functools.reduce(jnp.logical_and, tests)

    near = [
        (dx, dy)
        for dy in range(-4, 5)
        for dx in range(-2, 3)
        if (dx or dy) and abs(dx) * abs(dy) < 4 and (dx == 0 or abs(dy) < 4)
    ]
    for dx, dy in near:

        @pl.when(within(dx, dy))
        def _():
            pl.semaphore_signal(
                barrier, inc=1, device_id=device(dx, dy), device_id_type=MESH
            )

    present = sum(within(dx, dy).astype(jnp.int32) for dx, dy in near)

    locals_ = [
        pltpu.make_async_copy(source, target, local_sem.at[place])
        for place, (source, target) in enumerate(
            [
                (pinning_ref, pin),
                (lead_ref, lead),
                (along_z_ref, along_z),
                (along_x_ref, along_x),
                (along_y_ref, along_y),
                (inverse_ref, inverse),
                (back_x_ref.at[:, gx], back_x),
                (back_yz_ref.at[:, pl.ds(gy, 5)], back_yz),
            ]
        )
    ]
    for ref in (part0, pa0, pb0, part1, pa1, pb1, part2, pa2, pb2):
        ref[...] = jnp.zeros(ref.shape, jnp.float32)

    def clear(*refs):
        for ref in refs:
            ref[...] = jnp.zeros(ref.shape, jnp.float32)

    @pl.when(gx == 0)
    def _():
        clear(tile0.at[:, 0:3], low_in.at[:, 0:3], high_in.at[:, 0:3])
        clear(tile1.at[:, 0:4], got2.at[0:2])

    @pl.when(gx == 1)
    def _():
        clear(got2.at[0:1])

    @pl.when(gx == ngx - 1)
    def _():
        clear(tile0.at[:, 19:22], low_in.at[:, 19:22], high_in.at[:, 19:22])
        clear(tile1.at[:, 12:16], got2.at[3:5])

    @pl.when(gx == ngx - 2)
    def _():
        clear(got2.at[4:5])

    for place in range(3):

        @pl.when(gy == place)
        def _():
            clear(got2.at[:, 0 : 3 - place])

        @pl.when(gy == ngy - 1 - place)
        def _():
            clear(got2.at[:, 4 + place : 7])

    @pl.when(gy == 0)
    def _():
        clear(low_in, tile1.at[:, :, 0:8])

    @pl.when(gy == ngy - 1)
    def _():
        clear(high_in, tile1.at[:, :, 16:24])

    own_state.wait()
    face_out[0] = ext[:, 1:17, 8:9, :]
    face_out[1] = ext[:, 1:17, 15:16, :]
    pl.semaphore_wait(barrier, present)

    sent = []

    def push(source, target, dx, dy, sems, place):
        copy = pltpu.make_async_remote_copy(
            src_ref=source,
            dst_ref=target,
            send_sem=sems.at[0, place],
            recv_sem=sems.at[1, place],
            device_id=device(dx, dy),
            device_id_type=MESH,
        )
        outward = within(dx, dy)
        pl.when(outward)(lambda: copy.start())
        sent.append((copy, outward))
        return copy, within(-dx, -dy)

    def receive(copies):
        for copy, inward in copies:
            pl.when(inward)(lambda: copy.wait_recv())

    halo = [
        push(face_out.at[0], face_in.at[0], 0, -1, halo_sem, 0),
        push(face_out.at[1], face_in.at[1], 0, 1, halo_sem, 1),
        push(ext.at[:, 1, 8:16], ext.at[:, 17, 8:16], -1, 0, halo_sem, 2),
        push(ext.at[:, 16, 8:16], ext.at[:, 0, 8:16], 1, 0, halo_sem, 3),
        push(face_out.at[1, 3, 0], diag_in.at[0], -1, 1, halo_sem, 4),
        push(face_out.at[0, 2, 15], diag_in.at[1], 1, -1, halo_sem, 5),
    ]
    for copy in locals_:
        copy.start()

    def relays(reach, count):
        steps = []
        while reach < count - 1:
            steps.append(reach)
            reach *= 2
        return steps

    relays_x = [(reach, 0) for reach in relays(2, ngx)]
    relays_y = [(0, reach) for reach in relays(4, ngy)]

    def tell(steps, first, place):
        if place < len(steps):
            dx, dy = steps[place]
            for side, sign in enumerate((-1, 1)):

                @pl.when(within(sign * dx, sign * dy))
                def _():
                    pl.semaphore_signal(
                        relay_sem.at[first + place, side],
                        inc=1,
                        device_id=device(sign * dx, sign * dy),
                        device_id_type=MESH,
                    )

    def hear(steps, first, place):
        if place < len(steps):
            dx, dy = steps[place]
            for side, sign in enumerate((-1, 1)):

                @pl.when(within(-sign * dx, -sign * dy))
                def _():
                    pl.semaphore_wait(relay_sem.at[first + place, side], 1)

    tell(relays_y, 4, 0)
    tell(relays_x, 0, 0)

    lane = lax.broadcasted_iota(jnp.int32, (1, NZ), 1)
    row8 = lax.broadcasted_iota(jnp.int32, (TY, NZ), 0)

    def ahead_z(values):
        return jnp.where(lane == NZ - 1, 0.0, pltpu.roll(values, NZ - 1, 1))

    def behind_z(values):
        return jnp.where(lane == 0, 0.0, pltpu.roll(values, 1, 1))

    def here(field, slab, dx=0, dy=0):
        return ext[field, slab + (1 + dx), 8 + dy : 16 + dy, :]

    def link(c, s, re, im, next_re, next_im):
        moved_re = c * next_re + s * next_im
        moved_im = c * next_im - s * next_re
        current = re * moved_im - im * moved_re
        return moved_re, moved_im, c * re - s * im, c * im + s * re, current

    def own_part(i):
        re, im = here(0, i), here(1, i)
        c, s = cos_sin(here(4, i))
        moved_re, moved_im, back_re, back_im, current = link(
            c, s, re, im, ahead_z(re), ahead_z(im)
        )
        rates[0, i] = moved_re + behind_z(back_re)
        rates[1, i] = moved_im + behind_z(back_im)
        rates[4, i] = current
        work[0, i] = behind_z(current) - current
        work[1, i], work[2, i] = cos_sin(here(2, i))
        work[3, i], work[4, i] = cos_sin(here(3, i))

    each(0, TX, own_part)
    hear(relays_y, 4, 0)
    tell(relays_y, 4, 1)
    hear(relays_x, 0, 0)
    tell(relays_x, 0, 1)
    for copy in locals_:
        copy.wait()
    work[0, 0] += jnp.where(gx == 0, 1.0, 0.0) * lead[0]
    work[0, TX - 1] += jnp.where(gx == ngx - 1, 1.0, 0.0) * lead[1]

    receive(halo)
    ext[:, 1:17, 16:17, :] = face_in[0]
    ext[:, 1:17, 7:8, :] = face_in[1]
    ext[3, 17, 7:8, :] = diag_in[0]
    ext[2, 0, 16:17, :] = diag_in[1]

    @pl.when(gx == 0)
    def _():
        ext[:, 0, :, :] = jnp.zeros((5, 24, NZ), jnp.float32)

    @pl.when(gx == ngx - 1)
    def _():
        ext[:, 17, :, :] = jnp.zeros((5, 24, NZ), jnp.float32)

    @pl.when(gy == 0)
    def _():
        ext[:, :, 7:8, :] = jnp.zeros((5, 18, 1, NZ), jnp.float32)

    @pl.when(gy == ngy - 1)
    def _():
        ext[:, :, 16:17, :] = jnp.zeros((5, 18, 1, NZ), jnp.float32)

    def source_part(i, carry):
        from_re, from_im, from_current = carry
        re, im = here(0, i), here(1, i)
        moved_re, moved_im, back_re, back_im, current = link(
            work[1, i], work[2, i], re, im, here(0, i, 1), here(1, i, 1)
        )
        up_re, up_im, _, _, up_current = link(
            work[3, i], work[4, i], re, im, here(0, i, 0, 1), here(1, i, 0, 1)
        )
        c, s = cos_sin(here(3, i, 0, -1))
        _, _, down_re, down_im, down_current = link(
            c, s, here(0, i, 0, -1), here(1, i, 0, -1), re, im
        )
        rates[0, i] += (moved_re + from_re) + (up_re + down_re)
        rates[1, i] += (moved_im + from_im) + (up_im + down_im)
        rates[2, i] = current
        rates[3, i] = up_current
        source = work[0, i] - (current - from_current) - (up_current - down_current)
        tile0[0, i + 3] = source
        part0[i + 4, 4:12] = source
        low_out[0, i] = source[0:4]
        high_out[0, i] = source[4:8]
        return back_re, back_im, current

    c, s = cos_sin(here(2, -1))
    _, _, back_re, back_im, current = link(
        c, s, here(0, -1), here(1, -1), here(0, 0), here(1, 0)
    )
    lax.fori_loop(0, TX, source_part, (back_re, back_im, current), unroll=True)

    def exchange0(kind):
        tile, low, high = tile0.at[kind], low_out.at[kind], high_out.at[kind]
        low_to, high_to = low_in.at[kind], high_in.at[kind]
        sems = level0_sem.at[kind]
        return [
            push(low, high_to.at[3:19], 0, -1, sems, 0),
            push(high, low_to.at[3:19], 0, 1, sems, 1),
            push(tile.at[3:6], tile.at[19:22], -1, 0, sems, 2),
            push(tile.at[16:19], tile.at[0:3], 1, 0, sems, 3),
            push(low.at[0:3], high_to.at[19:22], -1, -1, sems, 4),
            push(low.at[13:16], high_to.at[0:3], 1, -1, sems, 5),
            push(high.at[0:3], low_to.at[19:22], -1, 1, sems, 6),
            push(high.at[13:16], low_to.at[0:3], 1, 1, sems, 7),
        ]

    def exchange1(kind):
        tile = tile1.at[kind]
        sems = level1_sem.at[kind]
        own = tile.at[4:12, 8:16]
        first, last = tile.at[4:8, 8:16], tile.at[8:12, 8:16]
        return [
            push(own, tile.at[4:12, 16:24], 0, -1, sems, 0),
            push(own, tile.at[4:12, 0:8], 0, 1, sems, 1),
            push(first, tile.at[12:16, 8:16], -1, 0, sems, 2),
            push(last, tile.at[0:4, 8:16], 1, 0, sems, 3),
            push(first, tile.at[12:16, 16:24], -1, -1, sems, 4),
            push(last, tile.at[0:4, 16:24], 1, -1, sems, 5),
            push(first, tile.at[12:16, 0:8], -1, 1, sems, 6),
            push(last, tile.at[0:4, 0:8], 1, 1, sems, 7),
        ]

    def exchange2():
        copies = []
        for dy in (-3, 3, -2, 2, -1, 1, 0):
            for dx in (-1, 1, 0, -2, 2):
                if (dx or dy) and (abs(dx) < 2 or abs(dy) < 2):
                    target = got2.at[2 - dx, 3 - dy]
                    copies.append(push(got2.at[2, 3], target, dx, dy, level2_sem, len(copies)))
        return copies

    def unpack2():
        for across in range(5):
            for place in range(7):
                if across in (0, 4) and abs(place - 3) > 1:
                    continue
                for x in range(4):
                    slab = 4 * across + x - 2
                    if 0 <= slab < 16:
                        src2[slab, 2 * place : 2 * place + 2] = got2[
                            across, place, 2 * x : 2 * x + 2
                        ]

    def assemble0(kind):
        def one(slab):
            src0[kind, slab, 0:4] = low_in[kind, slab]
            src0[kind, slab, 4:12] = tile0[kind, slab]
            src0[kind, slab, 12:16] = high_in[kind, slab]

        each(0, 22, one)

    level0 = (22, 16, 4, 8, 1, 1, 16, 3)
    level1 = (16, 24, 8, 8, 2, 2, 8, 4)
    level2 = (16, 16, 6, 2, 1, 4, 4, 6)
    spread0 = (24, 16, 4, 8, 1, 1, 16, 4)
    spread1 = (20, 16, 6, 4, 1, 2, 8, 6)
    spread2 = (20, 16, 6, 2, 1, 4, 4, 8)

    def inside(level, slab):
        place = gx * level[6] + (slab - level[7])
        return jnp.logical_and(place >= 0, place < ngx * level[6])

    def gain_at(level, slab):
        return jnp.where(inside(level, slab), GAIN, 0.0)

    def edge_masks(level, row, rows):
        own_row, own_rows, step = level[2:5]
        place = lax.broadcasted_iota(jnp.int32, (rows, NZ), 0) + (gy * own_rows + (row - own_row))
        at_top = jnp.logical_and(place >= ngy * own_rows - step, place < ngy * own_rows)
        at_low = jnp.logical_and(place >= 0, place < step)
        return at_top, at_low

    def around(level, masks, ref, slab, row, rows):
        step, lanes = level[4:6]
        row = row + 8
        centre = ref[slab, row : row + rows]
        above = jnp.where(masks[0], centre, ref[slab, row + step : row + step + rows])
        below = jnp.where(masks[1], centre, ref[slab, row - step : row - step + rows])
        right = jnp.where(lane >= NZ - lanes, centre, pltpu.roll(centre, NZ - lanes, 1))
        left = jnp.where(lane < lanes, centre, pltpu.roll(centre, lanes, 1))
        along = ref[slab + 1, row : row + rows] + ref[slab - 1, row : row + rows]
        return centre, along + (above + below) + (left + right)

    def sweep(level, ref, to, source, first, last):
        rows = level[1]
        masks = edge_masks(level, 0, rows)

        def one(slab):
            centre, total = around(level, masks, ref, slab, 0, rows)
            fresh = KEEP * centre + gain_at(level, slab) * (total + source[slab])
            to[slab, 8 : 8 + rows] = fresh

        each(first, last, one)

    def smooth_down(level, source, va, vb):
        slabs, rows = level[:2]

        def one(slab):
            va[slab, 8 : 8 + rows] = gain_at(level, slab) * source[slab]

        each(0, slabs, one)
        sweep(level, va, vb, source, 1, slabs - 1)
        sweep(level, vb, va, source, 2, slabs - 2)

    def restrict_to(level, source, ref, visit):
        row, _, step, lanes, tile, margin = level[2:8]
        masks = edge_masks(level, row, TY)
        odd_row = lax.rem(lax.div(row8, step), 2) == 1
        odd_lane = lax.rem(lax.div(lane, lanes), 2) == 1

        def rest(slab):
            centre, total = around(level, masks, ref, slab, row, TY)
            return source[slab, row : row + TY] + total - 6.0 * centre

        def one(pair):
            total = rest(margin + 2 * pair) + rest(margin + 1 + 2 * pair)
            total = total + jnp.where(
                odd_row, pltpu.roll(total, step, 0), pltpu.roll(total, TY - step, 0)
            )
            total = total + jnp.where(
                odd_lane, pltpu.roll(total, lanes, 1), pltpu.roll(total, NZ - lanes, 1)
            )
            visit(pair, 0.5 * total)

        each(0, tile // 2, one)

    def smooth_up(level, start, source, va, vb, first=0):
        slabs, rows = level[:2]

        def one(slab):
            va[slab, 8 : 8 + rows] = jnp.where(inside(level, slab), start(slab), 0.0)

        each(first, slabs - first, one)
        sweep(level, va, vb, source, first + 1, slabs - first - 1)
        sweep(level, vb, va, source, first + 2, slabs - first - 2)

    def spread_down(level, source, va, vb, first, last):
        slabs, rows = level[:2]

        def one(slab):
            va[slab, 8 : 8 + rows] = gain_at(level, slab) * source[slab]

        each(first, last, one)
        sweep(level, va, vb, source, first - 1, last + 1)
        sweep(level, vb, va, source, first - 2, last + 2)
        masks = edge_masks(level, 0, rows)

        def rest(slab):
            centre, total = around(level, masks, va, slab, 0, rows)
            return source[slab] + total - 6.0 * centre

        begin, end = first - 3, last + 3
        pairs = list(range(begin // 2, (end + 1) // 2))
        for pair in pairs:
            both = [rest(slab) for slab in (2 * pair, 2 * pair + 1) if begin <= slab < end]
            folded[pair] = both[0] + both[1] if len(both) == 2 else both[0]
        return pairs

    def fold(level, pairs, visit):
        lanes = level[5]
        odd_lane = lax.rem(lax.div(lane, lanes), 2) == 1
        for place, pair in enumerate(pairs):
            total = folded[pair, pl.ds(0, 8, 2)] + folded[pair, pl.ds(1, 8, 2)]
            total = total + jnp.where(
                odd_lane, pltpu.roll(total, lanes, 1), pltpu.roll(total, NZ - lanes, 1)
            )
            visit(place, 0.5 * total)

    near0 = exchange0(0)
    hear(relays_x, 0, 1)
    tell(relays_x, 0, 2)

    def to_part1(place, values):
        part1[place + 4, 4:12] = values

    def to_part2(place, values):
        part2[place + 5, 3:11] = values

    fold(spread0, spread_down(spread0, part0, pa0, pb0, 4, 20), to_part1)
    fold(spread1, spread_down(spread1, part1, pa1, pb1, 4, 16), to_part2)
    spread_down(spread2, part2, pa2, pb2, 5, 15)
    modes = product(
        halves(folded[1:9].reshape(8 * 16, NZ)), (along_z[0], along_z[1])
    ).reshape(8, 16, NZ)
    row16 = lax.broadcasted_iota(jnp.int32, (16, NZ), 0)
    lane16 = lax.div(lax.broadcasted_iota(jnp.int32, (16, NZ), 1), 16)
    group_of = lax.rem(gy + 5 + lax.div(row16, 2), 8)
    gather1[gy] = jnp.sum(jnp.where((lane16 == group_of)[None], modes, 0.0), axis=1)

    def spread(ref, mine, count, target, place):
        def one(step):
            return pltpu.make_async_remote_copy(
                src_ref=ref.at[mine],
                dst_ref=ref.at[mine],
                send_sem=gather_sem.at[0, place],
                recv_sem=gather_sem.at[1, place],
                device_id=target(lax.rem(mine + step, count)),
                device_id_type=MESH,
            )

        @pl.loop(0, count - 1)
        def _(turn):
            away = lax.div(turn + 1, 2)
            one(count // 2 + away * (2 * lax.rem(turn, 2) - 1)).start()

        rest_of = ref.at[0 : count - 1]
        return pltpu.make_async_remote_copy(
            src_ref=rest_of,
            dst_ref=rest_of,
            send_sem=gather_sem.at[0, place],
            recv_sem=gather_sem.at[1, place],
            device_id=target(lax.rem(mine + 1, count)),
            device_id_type=MESH,
        )

    hear(relays_y, 4, 1)
    along = spread(gather1, gy, ngy, lambda other: (gx, other), 0)
    hear(relays_x, 0, 2)
    tell(relays_x, 0, 3)

    def flux_xy(i, dx, dy):
        return (here(3, i, dx + 1, dy) - here(3, i, dx, dy)) - (
            here(2, i, dx, dy + 1) - here(2, i, dx, dy)
        )

    def flux_yz(i, dy):
        a_y = here(3, i, 0, dy)
        return (here(4, i, 0, dy + 1) - here(4, i, 0, dy)) - (ahead_z(a_y) - a_y)

    def flux_zx(i, dx):
        a_x = here(2, i, dx, 0)
        return (ahead_z(a_x) - a_x) - (here(4, i, dx + 1, 0) - here(4, i, dx, 0))

    def rate_part(i):
        re, im = here(0, i), here(1, i)
        condense = pin[i] - (re * re + im * im) - 6.0
        rates[0, i] += condense * re
        rates[1, i] += condense * im
        under_x = jnp.where(lane == 0, here(2, i), 0.0)
        under_y = jnp.where(lane == 0, here(3, i), 0.0)
        xy, yz, zx = flux_xy(i, 0, 0), flux_yz(i, 0), flux_zx(i, 0)
        rates[2, i] -= KAPPA2 * ((xy - flux_xy(i, 0, -1)) - (zx - (behind_z(zx) + under_x)))
        rates[3, i] -= KAPPA2 * ((yz - (behind_z(yz) - under_y)) - (xy - flux_xy(i, -1, 0)))
        rates[4, i] -= KAPPA2 * ((zx - flux_zx(i, -1)) - (yz - flux_yz(i, -1)))

    each(0, TX, rate_part)

    receive(near0)
    assemble0(0)
    smooth_down(level0, src0.at[0], va0, vb0)

    def to_level1(pair, values):
        tile1[0, pair + 4, 8:16] = values

    restrict_to(level0, src0.at[0], va0, to_level1)
    near1 = exchange1(0)

    def keep0(i):
        values = va0[i + 3, 12:20]
        tile0[1, i + 3] = values
        low_out[1, i] = values[0:4]
        high_out[1, i] = values[4:8]

    each(0, TX, keep0)
    late0 = exchange0(1)

    along.wait_recv()
    groups = max(1, ngy // 8)
    chip, core = lax.div(gx, 2), lax.rem(gx, 2)
    lane8 = lax.div(lax.broadcasted_iota(jnp.int32, (8, NZ), 1), 16)
    for group in range(groups):
        total = jnp.zeros((8, NZ), jnp.float32)
        for sender in range(ngy):
            low, high = sender - 3 - 8 * group, sender + 3 - 8 * group
            if high >= 0 and low < 8:
                held = jnp.logical_and(lane8 >= low, lane8 <= high)
                total = total + jnp.where(held, gather1[sender], 0.0)
        gather2[core, chip, :, 128 * group : 128 * group + 128] = total
    hear(relays_x, 0, 3)
    across = spread(
        gather2.at[core], chip, ngx // 2, lambda other: (2 * other + core, gy), 1
    )

    receive(near1)
    smooth_down(level1, tile1.at[0], va1, vb1)

    def to_level2(pair, values):
        got2[2, 3, pl.ds(2 * pair, 1)] = values[0:1]
        got2[2, 3, pl.ds(2 * pair + 1, 1)] = values[4:5]

    restrict_to(level1, tile1.at[0], va1, to_level2)
    near2 = exchange2()

    def keep1(i):
        tile1[1, i + 4, 8:16] = va1[i + 4, 16:24]

    each(0, 8, keep1)
    late1 = exchange1(1)

    across.wait_recv()
    swap = pltpu.make_async_remote_copy(
        src_ref=gather2.at[core],
        dst_ref=gather2.at[core],
        send_sem=gather_sem.at[0, 2],
        recv_sem=gather_sem.at[1, 2],
        device_id=(gx + 1 - 2 * core, gy),
        device_id_type=MESH,
    )
    swap.start()
    swap.wait_recv()
    shares = gather2[...].reshape(8 * ngx, 128 * groups)
    spectral = product((along_x[0], along_x[1]), halves(shares))
    spectral = product(halves(spectral), (along_y[0], along_y[1])) * inverse[...]
    spectral = product((back_x[0, :, : 2 * ngx], back_x[1, :, : 2 * ngx]), halves(spectral))
    spectral = halves(spectral)
    for place in range(5):
        column = product(spectral, (back_yz[0, place], back_yz[1, place]))
        for x in range(6):
            coarse[x, 2 * place + 2 : 2 * place + 4] = column[2 * x : 2 * x + 2]

    receive(near2)
    unpack2()
    smooth_down(level2, src2, va2, vb2)
    smooth_up(
        level2,
        lambda slab: va2[slab, 8:24] + coarse[lax.div(slab, 2) - 1],
        src2,
        va2,
        vb2,
        first=2,
    )
    receive(late1)

    def start1(slab):
        x = lax.div(slab, 2) + 4
        parts = []
        for place in range(3):
            row = 12 + 2 * place
            parts.append(jnp.where(row8 < 4, va2[x, row : row + 1], va2[x, row + 1 : row + 2]))
        return tile1[1, slab] + jnp.concatenate(parts, 0)

    smooth_up(level1, start1, tile1.at[0], va1, vb1)
    receive(late0)
    assemble0(1)
    smooth_up(
        level0,
        lambda slab: src0[1, slab] + va1[lax.div(slab + 1, 2) + 2, 12:28],
        src0.at[0],
        va0,
        vb0,
    )

    not_top = jnp.logical_or(row8 < TY - 1, gy < ngy - 1)

    def finish(i):
        potential = va0[i + 3, 12:20]
        above = jnp.where(not_top, va0[i + 3, 13:21], 0.0)
        potential_ref[i] = potential
        re, im = here(0, i), here(1, i)
        out_ref[0, i] = re + DT * (rates[0, i] + potential * im)
        out_ref[1, i] = im + DT * (rates[1, i] - potential * re)
        out_ref[2, i] = here(2, i) + DT * (rates[2, i] - (va0[i + 4, 12:20] - potential))
        out_ref[3, i] = here(3, i) + DT * (rates[3, i] - (above - potential))
        out_ref[4, i] = here(4, i) + DT * (rates[4, i] - (ahead_z(potential) - potential))

    each(0, TX, finish)

    for copy, outward in sent:
        pl.when(outward)(lambda: copy.wait_send())
    along.wait_send()
    across.wait_send()
    swap.wait_send()


def solution(mesh):
    ngx, ngy = mesh.shape["gx"], mesh.shape["gy"]
    tables = coarse_tables(ngx, ngy)
    groups = max(1, ngy // 8)
    width = 128 * groups
    f32, bf16 = jnp.float32, jnp.bfloat16
    vmem, dma = pltpu.VMEM, pltpu.SemaphoreType.DMA

    def body(state, pinning, lead_values):
        return pl.pallas_call(
            functools.partial(kernel, ngx, ngy),
            out_shape=(vmem(state.shape, f32), vmem(pinning.shape, f32)),
            in_specs=[pl.BlockSpec(memory_space=pltpu.HBM)] * 9,
            out_specs=(
                pl.BlockSpec(memory_space=pltpu.VMEM),
                pl.BlockSpec(memory_space=pltpu.VMEM),
            ),
            scratch_shapes=[
                vmem((5, TX + 2, 24, NZ), f32),
                vmem((TX, TY, NZ), f32),
                vmem((2, TY, NZ), f32),
                vmem(tables[0].shape, bf16),
                vmem(tables[1].shape, bf16),
                vmem(tables[2].shape, bf16),
                vmem(tables[3].shape, f32),
                vmem((2, 16, 128), bf16),
                vmem((2, 5, width, 128), bf16),
                vmem((2, 5, TX, 1, NZ), f32),
                vmem((2, 5, TX, 1, NZ), f32),
                vmem((2, 1, NZ), f32),
                vmem((5, TX, TY, NZ), f32),
                vmem((5, TX, TY, NZ), f32),
                vmem((2, 22, TY, NZ), f32),
                vmem((2, TX, 4, NZ), f32),
                vmem((2, TX, 4, NZ), f32),
                vmem((2, 22, 4, NZ), f32),
                vmem((2, 22, 4, NZ), f32),
                vmem((2, 22, 16, NZ), f32),
                vmem((22, 32, NZ), f32),
                vmem((22, 32, NZ), f32),
                vmem((2, 16, 24, NZ), f32),
                vmem((16, 40, NZ), f32),
                vmem((16, 40, NZ), f32),
                vmem((5, 7, TY, NZ), f32),
                vmem((16, 16, NZ), f32),
                vmem((16, 32, NZ), f32),
                vmem((16, 32, NZ), f32),
                vmem((24, 16, NZ), f32),
                vmem((24, 32, NZ), f32),
                vmem((24, 32, NZ), f32),
                vmem((20, 16, NZ), f32),
                vmem((20, 32, NZ), f32),
                vmem((20, 32, NZ), f32),
                vmem((20, 16, NZ), f32),
                vmem((20, 32, NZ), f32),
                vmem((20, 32, NZ), f32),
                vmem((12, 16, NZ), f32),
                vmem((6, 16, NZ), f32),
                vmem((ngy, 8, NZ), f32),
                vmem((2, ngx // 2, 8, width), f32),
                dma((8,)),
                dma,
                dma((2, 6)),
                dma((2, 2, 8)),
                dma((2, 2, 8)),
                dma((2, 26)),
                dma((2, 3)),
                pltpu.SemaphoreType.REGULAR((6, 2)),
            ],
            compiler_params=pltpu.CompilerParams(
                collective_id=0, has_side_effects=True, vmem_limit_bytes=60 * 1024 * 1024
            ),
            name="film_step",
        )(state, pinning, lead_values, *[jnp.asarray(table) for table in tables])
    placed = (P(None, "gx", "gy", None), P("gx", "gy", None), P(None, "gy", None))
    return jax.shard_map(
        body,
        mesh=mesh,
        in_specs=placed,
        out_specs=(P(None, "gx", "gy", None), P("gx", "gy", None)),
        check_vma=False,
    )
```

time: 465 us -> 43.8 us (0.09)
  the two profiles are of different devices: /device:TPU:100 before, /device:TPU:1 now
where the time goes in v1:
time: 43.8 us; the launch traced here: 43.7 us
  Pallas kernels  41.7 us (95%)
  local copies, waits for them, and re-layouts  1.36 us (3%)
  between operations  0.64 us (1%)
    pallas_call x1, Pallas kernels, body(): pl.pallas_call(functools.partial(kernel, ngx, ngy), out_shape=(vmem(state...  41.7 us
    unnamed x2, local copies, waits for them, and re-layouts  1.36 us

profile of v1, /device:TPU:1, one launch (start us, length us, event | category | flops | bytes accessed | tf_op | source)
XLA Modules:
  0.0 43.7 jit_solution(17349162753674042285)
XLA Ops:
  0.6 41.7 %film_step.1 = (f32[5,16,8,128]{3,2,1,0:T(8,128)S(1)}, f32[16,8,128]{2,1,0:T(8,128)S(1)}) custom-call(f32[5,16,8,128]{3,2,1,0:T(8,128)} %state_ref.1, f32[16,8,128]{2,1,0:T(8,128)} %pinning_ref.1, f32[2,8,128]{2,1,0:T(8,128)} %lead_ref.1, bf16[2,128,128]{2,1,0:T(8,128)(2,1)} %constant.12.clone.along_z_ref, bf16[2,64,256]{2,1,0:T(8,128)(2,1)} %constant.13.clone.along_x_ref, ...), custom_call_target="tpu_custom_call" | custom-call | tf_op jit(solution)/shard_map/film_step/pallas_call | solution.py:838
  42.3 0.7 %copy.13 = f32[5,16,8,128]{3,2,1,0:T(8,128)} copy(f32[5,16,8,128]{3,2,1,0:T(8,128)S(1)} %get-tuple-element.2) | data formatting | bytes 655360
  43.0 0.6 %copy.14 = f32[16,8,128]{2,1,0:T(8,128)} copy(f32[16,8,128]{2,1,0:T(8,128)S(1)} %get-tuple-element.3) | data formatting | bytes 131072

commit v2 on v1

--- a/solution.py
+++ b/solution.py
@@ -158,6 +158,8 @@
     tile1,
     va1,
     vb1,
+    share,
+    got_share,
     got2,
     src2,
     va2,
@@ -180,6 +182,7 @@
     halo_sem,
     level0_sem,
     level1_sem,
+    share_sem,
     level2_sem,
     gather_sem,
     relay_sem,
@@ -198,6 +201,7 @@
 
     own_state = pltpu.make_async_copy(state_ref, ext.at[:, 1:17, 8:16], state_sem)
     own_state.start()
+    got_share[...] = jnp.zeros(got_share.shape, jnp.float32)
     barrier = pltpu.get_barrier_semaphore()
     def within(dx, dy):
         tests = [gx >= -dx] * (dx < 0) + [gx < ngx - dx] * (dx > 0)
@@ -432,7 +436,7 @@
         rates[3, i] = up_current
         source = work[0, i] - (current - from_current) - (up_current - down_current)
         tile0[0, i + 3] = source
-        part0[i + 4, 4:12] = source
+        part0[i + 4, 12:20] = source
         low_out[0, i] = source[0:4]
         high_out[0, i] = source[4:8]
         return back_re, back_im, current
@@ -589,19 +593,21 @@
         sweep(level, vb, va, source, first + 2, slabs - first - 2)
 
     def spread_down(level, source, va, vb, first, last):
-        slabs, rows = level[:2]
-
-        def one(slab):
-            va[slab, 8 : 8 + rows] = gain_at(level, slab) * source[slab]
-
-        each(first, last, one)
-        sweep(level, va, vb, source, first - 1, last + 1)
-        sweep(level, vb, va, source, first - 2, last + 2)
+        rows = level[1]
         masks = edge_masks(level, 0, rows)
+        inner = source.at[:, 8 : 8 + rows]
+
+        def two(slab):
+            centre, total = around(level, masks, source, slab, 0, rows)
+            fresh = gain_at(level, slab) * ((1.0 + KEEP) * centre + GAIN * total)
+            vb[slab, 8 : 8 + rows] = fresh
+
+        each(first - 1, last + 1, two)
+        sweep(level, vb, va, inner, first - 2, last + 2)
 
         def rest(slab):
             centre, total = around(level, masks, va, slab, 0, rows)
-            return source[slab] + total - 6.0 * centre
+            return inner[slab] + total - 6.0 * centre
 
         begin, end = first - 3, last + 3
         pairs = list(range(begin // 2, (end + 1) // 2))
@@ -618,17 +624,20 @@
             total = total + jnp.where(
                 odd_lane, pltpu.roll(total, lanes, 1), pltpu.roll(total, NZ - lanes, 1)
             )
-            visit(place, 0.5 * total)
+            visit(place, total)
 
     near0 = exchange0(0)
     hear(relays_x, 0, 1)
     tell(relays_x, 0, 2)
 
+    def half_at(level, slab):
+        return jnp.where(inside(level, slab), 0.5, 0.0)
+
     def to_part1(place, values):
-        part1[place + 4, 4:12] = values
+        part1[place + 4, 12:20] = half_at(spread1, place + 4) * values
 
     def to_part2(place, values):
-        part2[place + 5, 3:11] = values
+        part2[place + 5, 11:19] = half_at(spread2, place + 5) * values
 
     fold(spread0, spread_down(spread0, part0, pa0, pb0, 4, 20), to_part1)
     fold(spread1, spread_down(spread1, part1, pa1, pb1, 4, 16), to_part2)
@@ -671,6 +680,35 @@
     along = spread(gather1, gy, ngy, lambda other: (gx, other), 0)
     hear(relays_x, 0, 2)
     tell(relays_x, 0, 3)
+
+    around2 = [(dx, dy) for dy in range(-2, 3) for dx in range(-1, 2)]
+    for dx, dy in around2:
+        for x in range(4):
+            share[dx + 1, dy + 2, 2 * x : 2 * x + 2] = part2[
+                4 * dx + x + 8, 2 * dy + 14 : 2 * dy + 16
+            ]
+    shared = [
+        push(share.at[1 + dx, 2 + dy], got_share.at[1 - dx, 2 - dy], dx, dy, share_sem, place)
+        for place, (dx, dy) in enumerate(pair for pair in around2 if pair != (0, 0))
+    ]
+
+    receive(near0)
+    assemble0(0)
+    smooth_down(level0, src0.at[0], va0, vb0)
+
+    def to_level1(pair, values):
+        tile1[0, pair + 4, 8:16] = values
+
+    restrict_to(level0, src0.at[0], va0, to_level1)
+    near1 = exchange1(0)
+
+    receive(shared)
+    total = share[1, 2]
+    for dx, dy in around2:
+        if dx or dy:
+            total = total + got_share[1 + dx, 2 + dy]
+    got2[2, 3] = total
+    near2 = exchange2()
 
     def flux_xy(i, dx, dy):
         return (here(3, i, dx + 1, dy) - here(3, i, dx, dy)) - (
@@ -698,25 +736,6 @@
         rates[4, i] -= KAPPA2 * ((zx - flux_zx(i, -1)) - (yz - flux_yz(i, -1)))
 
     each(0, TX, rate_part)
-
-    receive(near0)
-    assemble0(0)
-    smooth_down(level0, src0.at[0], va0, vb0)
-
-    def to_level1(pair, values):
-        tile1[0, pair + 4, 8:16] = values
-
-    restrict_to(level0, src0.at[0], va0, to_level1)
-    near1 = exchange1(0)
-
-    def keep0(i):
-        values = va0[i + 3, 12:20]
-        tile0[1, i + 3] = values
-        low_out[1, i] = values[0:4]
-        high_out[1, i] = values[4:8]
-
-    each(0, TX, keep0)
-    late0 = exchange0(1)
 
     along.wait_recv()
     groups = max(1, ngy // 8)
@@ -735,21 +754,26 @@
         gather2.at[core], chip, ngx // 2, lambda other: (2 * other + core, gy), 1
     )
 
+    def keep0(i):
+        values = va0[i + 3, 12:20]
+        tile0[1, i + 3] = values
+        low_out[1, i] = values[0:4]
+        high_out[1, i] = values[4:8]
+
+    each(0, TX, keep0)
+    late0 = exchange0(1)
+
     receive(near1)
     smooth_down(level1, tile1.at[0], va1, vb1)
 
-    def to_level2(pair, values):
-        got2[2, 3, pl.ds(2 * pair, 1)] = values[0:1]
-        got2[2, 3, pl.ds(2 * pair + 1, 1)] = values[4:5]
-
-    restrict_to(level1, tile1.at[0], va1, to_level2)
-    near2 = exchange2()
-
     def keep1(i):
         tile1[1, i + 4, 8:16] = va1[i + 4, 16:24]
 
     each(0, 8, keep1)
     late1 = exchange1(1)
+    receive(near2)
+    unpack2()
+    smooth_down(level2, src2, va2, vb2)
 
     across.wait_recv()
     swap = pltpu.make_async_remote_copy(
@@ -772,9 +796,6 @@
         for x in range(6):
             coarse[x, 2 * place + 2 : 2 * place + 4] = column[2 * x : 2 * x + 2]
 
-    receive(near2)
-    unpack2()
-    smooth_down(level2, src2, va2, vb2)
     smooth_up(
         level2,
         lambda slab: va2[slab, 8:24] + coarse[lax.div(slab, 2) - 1],
@@ -869,17 +890,19 @@
                 vmem((2, 16, 24, NZ), f32),
                 vmem((16, 40, NZ), f32),
                 vmem((16, 40, NZ), f32),
+                vmem((3, 5, TY, NZ), f32),
+                vmem((3, 5, TY, NZ), f32),
                 vmem((5, 7, TY, NZ), f32),
                 vmem((16, 16, NZ), f32),
                 vmem((16, 32, NZ), f32),
                 vmem((16, 32, NZ), f32),
-                vmem((24, 16, NZ), f32),
                 vmem((24, 32, NZ), f32),
                 vmem((24, 32, NZ), f32),
-                vmem((20, 16, NZ), f32),
+                vmem((24, 32, NZ), f32),
                 vmem((20, 32, NZ), f32),
                 vmem((20, 32, NZ), f32),
-                vmem((20, 16, NZ), f32),
+                vmem((20, 32, NZ), f32),
+                vmem((20, 32, NZ), f32),
                 vmem((20, 32, NZ), f32),
                 vmem((20, 32, NZ), f32),
                 vmem((12, 16, NZ), f32),
@@ -891,6 +914,7 @@
                 dma((2, 6)),
                 dma((2, 2, 8)),
                 dma((2, 2, 8)),
+                dma((2, 14)),
                 dma((2, 26)),
                 dma((2, 3)),
                 pltpu.SemaphoreType.REGULAR((6, 2)),

time: 43.8 us -> 43.5 us (level)
  no operation moved by 1% of the time
where the time goes in v2:
time: 43.5 us; the launch traced here: 43.4 us
  Pallas kernels  41.4 us (95%)
  local copies, waits for them, and re-layouts  1.36 us (3%)
  between operations  0.64 us (1%)
    pallas_call x1, Pallas kernels, body(): pl.pallas_call(functools.partial(kernel, ngx, ngy), out_shape=(vmem(state...  41.4 us
    unnamed x2, local copies, waits for them, and re-layouts  1.36 us

profile of v2, /device:TPU:1, one launch (start us, length us, event | category | flops | bytes accessed | tf_op | source)
XLA Modules:
  0.0 43.4 jit_solution(6828518975887097860)
XLA Ops:
  0.6 41.4 %film_step.1 = (f32[5,16,8,128]{3,2,1,0:T(8,128)S(1)}, f32[16,8,128]{2,1,0:T(8,128)S(1)}) custom-call(f32[5,16,8,128]{3,2,1,0:T(8,128)} %state_ref.1, f32[16,8,128]{2,1,0:T(8,128)} %pinning_ref.1, f32[2,8,128]{2,1,0:T(8,128)} %lead_ref.1, bf16[2,128,128]{2,1,0:T(8,128)(2,1)} %constant.12.clone.along_z_ref, bf16[2,64,256]{2,1,0:T(8,128)(2,1)} %constant.13.clone.along_x_ref, ...), custom_call_target="tpu_custom_call" | custom-call | tf_op jit(solution)/shard_map/film_step/pallas_call | solution.py:859
  42.0 0.7 %copy.13 = f32[5,16,8,128]{3,2,1,0:T(8,128)} copy(f32[5,16,8,128]{3,2,1,0:T(8,128)S(1)} %get-tuple-element.2) | data formatting | bytes 655360
  42.8 0.6 %copy.14 = f32[16,8,128]{2,1,0:T(8,128)} copy(f32[16,8,128]{2,1,0:T(8,128)S(1)} %get-tuple-element.3) | data formatting | bytes 131072

commit v3 on v2

--- a/solution.py
+++ b/solution.py
@@ -155,6 +155,7 @@
     src0,
     va0,
     vb0,
+    got1,
     tile1,
     va1,
     vb1,
@@ -239,49 +240,6 @@
             ]
         )
     ]
-    for ref in (part0, pa0, pb0, part1, pa1, pb1, part2, pa2, pb2):
-        ref[...] = jnp.zeros(ref.shape, jnp.float32)
-
-    def clear(*refs):
-        for ref in refs:
-            ref[...] = jnp.zeros(ref.shape, jnp.float32)
-
-    @pl.when(gx == 0)
-    def _():
-        clear(tile0.at[:, 0:3], low_in.at[:, 0:3], high_in.at[:, 0:3])
-        clear(tile1.at[:, 0:4], got2.at[0:2])
-
-    @pl.when(gx == 1)
-    def _():
-        clear(got2.at[0:1])
-
-    @pl.when(gx == ngx - 1)
-    def _():
-        clear(tile0.at[:, 19:22], low_in.at[:, 19:22], high_in.at[:, 19:22])
-        clear(tile1.at[:, 12:16], got2.at[3:5])
-
-    @pl.when(gx == ngx - 2)
-    def _():
-        clear(got2.at[4:5])
-
-    for place in range(3):
-
-        @pl.when(gy == place)
-        def _():
-            clear(got2.at[:, 0 : 3 - place])
-
-        @pl.when(gy == ngy - 1 - place)
-        def _():
-            clear(got2.at[:, 4 + place : 7])
-
-    @pl.when(gy == 0)
-    def _():
-        clear(low_in, tile1.at[:, :, 0:8])
-
-    @pl.when(gy == ngy - 1)
-    def _():
-        clear(high_in, tile1.at[:, :, 16:24])
-
     own_state.wait()
     face_out[0] = ext[:, 1:17, 8:9, :]
     face_out[1] = ext[:, 1:17, 15:16, :]
@@ -317,6 +275,49 @@
     ]
     for copy in locals_:
         copy.start()
+
+    for ref in (part0, pa0, pb0, part1, pa1, pb1, part2, pa2, pb2):
+        ref[...] = jnp.zeros(ref.shape, jnp.float32)
+
+    def clear(*refs):
+        for ref in refs:
+            ref[...] = jnp.zeros(ref.shape, jnp.float32)
+
+    @pl.when(gx == 0)
+    def _():
+        clear(tile0.at[:, 0:3], low_in.at[:, 0:3], high_in.at[:, 0:3])
+        clear(got1.at[:, :, 0:1], got2.at[0:2])
+
+    @pl.when(gx == 1)
+    def _():
+        clear(got2.at[0:1])
+
+    @pl.when(gx == ngx - 1)
+    def _():
+        clear(tile0.at[:, 19:22], low_in.at[:, 19:22], high_in.at[:, 19:22])
+        clear(got1.at[:, :, 3:4], got2.at[3:5])
+
+    @pl.when(gx == ngx - 2)
+    def _():
+        clear(got2.at[4:5])
+
+    for place in range(3):
+
+        @pl.when(gy == place)
+        def _():
+            clear(got2.at[:, 0 : 3 - place])
+
+        @pl.when(gy == ngy - 1 - place)
+        def _():
+            clear(got2.at[:, 4 + place : 7])
+
+    @pl.when(gy == 0)
+    def _():
+        clear(low_in, got1.at[:, 0:1])
+
+    @pl.when(gy == ngy - 1)
+    def _():
+        clear(high_in, got1.at[:, 2:3])
 
     def relays(reach, count):
         steps = []
@@ -462,21 +463,44 @@
             push(high.at[13:16], low_to.at[0:3], 1, 1, sems, 7),
         ]
 
+    odd_row1, odd_lane1 = lax.rem(row8, 2) == 1, lax.rem(lane, 2) == 1
+
     def exchange1(kind):
-        tile = tile1.at[kind]
+        for half in range(2):
+            a, b, c, d = (tile1[kind, 4 + 4 * half + x, 8:16] for x in range(4))
+            got1[kind, 1, 1 + half] = jnp.where(
+                odd_row1, jnp.where(odd_lane1, d, c), jnp.where(odd_lane1, b, a)
+            )
+        got = got1.at[kind]
         sems = level1_sem.at[kind]
-        own = tile.at[4:12, 8:16]
-        first, last = tile.at[4:8, 8:16], tile.at[8:12, 8:16]
+        first, last = got.at[1, 1], got.at[1, 2]
         return [
-            push(own, tile.at[4:12, 16:24], 0, -1, sems, 0),
-            push(own, tile.at[4:12, 0:8], 0, 1, sems, 1),
-            push(first, tile.at[12:16, 8:16], -1, 0, sems, 2),
-            push(last, tile.at[0:4, 8:16], 1, 0, sems, 3),
-            push(first, tile.at[12:16, 16:24], -1, -1, sems, 4),
-            push(last, tile.at[0:4, 16:24], 1, -1, sems, 5),
-            push(first, tile.at[12:16, 0:8], -1, 1, sems, 6),
-            push(last, tile.at[0:4, 0:8], 1, 1, sems, 7),
+            push(got.at[1, 1:3], got.at[2, 1:3], 0, -1, sems, 0),
+            push(got.at[1, 1:3], got.at[0, 1:3], 0, 1, sems, 1),
+            push(first, got.at[1, 3], -1, 0, sems, 2),
+            push(last, got.at[1, 0], 1, 0, sems, 3),
+            push(first, got.at[2, 3], -1, -1, sems, 4),
+            push(last, got.at[2, 0], 1, -1, sems, 5),
+            push(first, got.at[0, 3], -1, 1, sems, 6),
+            push(last, got.at[0, 0], 1, 1, sems, 7),
         ]
+
+    def unpack1(kind):
+        for place in range(3):
+            for column in range(4):
+                if place == 1 and column in (1, 2):
+                    continue
+                packed = got1[kind, place, column]
+                even = jnp.where(odd_lane1, pltpu.roll(packed, 1, 1), packed)
+                odd = jnp.where(odd_lane1, packed, pltpu.roll(packed, NZ - 1, 1))
+                for x, values in enumerate((even, odd)):
+                    rows = slice(8 * place, 8 * place + 8)
+                    tile1[kind, 4 * column + x, rows] = jnp.where(
+                        odd_row1, pltpu.roll(values, 1, 0), values
+                    )
+                    tile1[kind, 4 * column + 2 + x, rows] = jnp.where(
+                        odd_row1, values, pltpu.roll(values, TY - 1, 0)
+                    )
 
     def exchange2():
         copies = []
@@ -701,41 +725,6 @@
 
     restrict_to(level0, src0.at[0], va0, to_level1)
     near1 = exchange1(0)
-
-    receive(shared)
-    total = share[1, 2]
-    for dx, dy in around2:
-        if dx or dy:
-            total = total + got_share[1 + dx, 2 + dy]
-    got2[2, 3] = total
-    near2 = exchange2()
-
-    def flux_xy(i, dx, dy):
-        return (here(3, i, dx + 1, dy) - here(3, i, dx, dy)) - (
-            here(2, i, dx, dy + 1) - here(2, i, dx, dy)
-        )
-
-    def flux_yz(i, dy):
-        a_y = here(3, i, 0, dy)
-        return (here(4, i, 0, dy + 1) - here(4, i, 0, dy)) - (ahead_z(a_y) - a_y)
-
-    def flux_zx(i, dx):
-        a_x = here(2, i, dx, 0)
-        return (ahead_z(a_x) - a_x) - (here(4, i, dx + 1, 0) - here(4, i, dx, 0))
-
-    def rate_part(i):
-        re, im = here(0, i), here(1, i)
-        condense = pin[i] - (re * re + im * im) - 6.0
-        rates[0, i] += condense * re
-        rates[1, i] += condense * im
-        under_x = jnp.where(lane == 0, here(2, i), 0.0)
-        under_y = jnp.where(lane == 0, here(3, i), 0.0)
-        xy, yz, zx = flux_xy(i, 0, 0), flux_yz(i, 0), flux_zx(i, 0)
-        rates[2, i] -= KAPPA2 * ((xy - flux_xy(i, 0, -1)) - (zx - (behind_z(zx) + under_x)))
-        rates[3, i] -= KAPPA2 * ((yz - (behind_z(yz) - under_y)) - (xy - flux_xy(i, -1, 0)))
-        rates[4, i] -= KAPPA2 * ((zx - flux_zx(i, -1)) - (yz - flux_yz(i, -1)))
-
-    each(0, TX, rate_part)
 
     along.wait_recv()
     groups = max(1, ngy // 8)
@@ -754,6 +743,50 @@
         gather2.at[core], chip, ngx // 2, lambda other: (2 * other + core, gy), 1
     )
 
+    receive(shared)
+    total = share[1, 2]
+    for dx, dy in around2:
+        if dx or dy:
+            total = total + got_share[1 + dx, 2 + dy]
+    got2[2, 3] = total
+    near2 = exchange2()
+
+    receive(near1)
+    unpack1(0)
+    smooth_down(level1, tile1.at[0], va1, vb1)
+
+    def keep1(i):
+        tile1[1, i + 4, 8:16] = va1[i + 4, 16:24]
+
+    each(0, 8, keep1)
+    late1 = exchange1(1)
+    def flux_xy(i, dx, dy):
+        return (here(3, i, dx + 1, dy) - here(3, i, dx, dy)) - (
+            here(2, i, dx, dy + 1) - here(2, i, dx, dy)
+        )
+
+    def flux_yz(i, dy):
+        a_y = here(3, i, 0, dy)
+        return (here(4, i, 0, dy + 1) - here(4, i, 0, dy)) - (ahead_z(a_y) - a_y)
+
+    def flux_zx(i, dx):
+        a_x = here(2, i, dx, 0)
+        return (ahead_z(a_x) - a_x) - (here(4, i, dx + 1, 0) - here(4, i, dx, 0))
+
+    def rate_part(i):
+        re, im = here(0, i), here(1, i)
+        condense = pin[i] - (re * re + im * im) - 6.0
+        rates[0, i] += condense * re
+        rates[1, i] += condense * im
+        under_x = jnp.where(lane == 0, here(2, i), 0.0)
+        under_y = jnp.where(lane == 0, here(3, i), 0.0)
+        xy, yz, zx = flux_xy(i, 0, 0), flux_yz(i, 0), flux_zx(i, 0)
+        rates[2, i] -= KAPPA2 * ((xy - flux_xy(i, 0, -1)) - (zx - (behind_z(zx) + under_x)))
+        rates[3, i] -= KAPPA2 * ((yz - (behind_z(yz) - under_y)) - (xy - flux_xy(i, -1, 0)))
+        rates[4, i] -= KAPPA2 * ((zx - flux_zx(i, -1)) - (yz - flux_yz(i, -1)))
+
+    each(0, TX, rate_part)
+
     def keep0(i):
         values = va0[i + 3, 12:20]
         tile0[1, i + 3] = values
@@ -762,18 +795,6 @@
 
     each(0, TX, keep0)
     late0 = exchange0(1)
-
-    receive(near1)
-    smooth_down(level1, tile1.at[0], va1, vb1)
-
-    def keep1(i):
-        tile1[1, i + 4, 8:16] = va1[i + 4, 16:24]
-
-    each(0, 8, keep1)
-    late1 = exchange1(1)
-    receive(near2)
-    unpack2()
-    smooth_down(level2, src2, va2, vb2)
 
     across.wait_recv()
     swap = pltpu.make_async_remote_copy(
@@ -785,6 +806,9 @@
         device_id_type=MESH,
     )
     swap.start()
+    receive(near2)
+    unpack2()
+    smooth_down(level2, src2, va2, vb2)
     swap.wait_recv()
     shares = gather2[...].reshape(8 * ngx, 128 * groups)
     spectral = product((along_x[0], along_x[1]), halves(shares))
@@ -805,6 +829,7 @@
         first=2,
     )
     receive(late1)
+    unpack1(1)
 
     def start1(slab):
         x = lax.div(slab, 2) + 4
@@ -847,6 +872,18 @@
     swap.wait_send()
 
 
+def hand_over(state_ref, potential_ref, out_ref, out_potential_ref, sems):
+    copies = [
+        pltpu.make_async_copy(state_ref.at[field], out_ref.at[field], sems.at[field])
+        for field in range(5)
+    ]
+    copies.append(pltpu.make_async_copy(potential_ref, out_potential_ref, sems.at[5]))
+    for copy in copies:
+        copy.start()
+    for copy in copies:
+        copy.wait()
+
+
 def solution(mesh):
     ngx, ngy = mesh.shape["gx"], mesh.shape["gy"]
     tables = coarse_tables(ngx, ngy)
@@ -856,7 +893,7 @@
     vmem, dma = pltpu.VMEM, pltpu.SemaphoreType.DMA
 
     def body(state, pinning, lead_values):
-        return pl.pallas_call(
+        stepped = pl.pallas_call(
             functools.partial(kernel, ngx, ngy),
             out_shape=(vmem(state.shape, f32), vmem(pinning.shape, f32)),
             in_specs=[pl.BlockSpec(memory_space=pltpu.HBM)] * 9,
@@ -887,6 +924,7 @@
                 vmem((2, 22, 16, NZ), f32),
                 vmem((22, 32, NZ), f32),
                 vmem((22, 32, NZ), f32),
+                vmem((2, 3, 4, TY, NZ), f32),
                 vmem((2, 16, 24, NZ), f32),
                 vmem((16, 40, NZ), f32),
                 vmem((16, 40, NZ), f32),
@@ -924,6 +962,18 @@
             ),
             name="film_step",
         )(state, pinning, lead_values, *[jnp.asarray(table) for table in tables])
+        return pl.pallas_call(
+            hand_over,
+            out_shape=(
+                jax.ShapeDtypeStruct(state.shape, f32),
+                jax.ShapeDtypeStruct(pinning.shape, f32),
+            ),
+            in_specs=[pl.BlockSpec(memory_space=pl.ANY)] * 2,
+            out_specs=[pl.BlockSpec(memory_space=pl.ANY)] * 2,
+            scratch_shapes=[dma((6,))],
+            compiler_params=pltpu.CompilerParams(vmem_limit_bytes=4 * 1024 * 1024),
+            name="hand_over",
+        )(*stepped)
     placed = (P(None, "gx", "gy", None), P("gx", "gy", None), P(None, "gy", None))
     return jax.shard_map(
         body,

time: 43.5 us -> 43.3 us (level)
  local copies, waits for them, and re-layouts: 1.36 us -> 0 us
  Pallas kernels: 41.4 us -> 42.5 us
    unnamed x2 -> x0, local copies, waits for them, and re-layouts: 1.36 us -> none
    pallas_call x0 -> x1, Pallas kernels: none -> 0.79 us  [body(): pl.pallas_call(hand_over, out_shape=(jax.ShapeDtypeStruct(state.shape, f3...]
where the time goes in v3:
time: 43.3 us; the launch traced here: 43.1 us
  Pallas kernels  42.5 us (98%)
  between operations  0.64 us (1%)
    pallas_call x1, Pallas kernels, body(): pl.pallas_call(functools.partial(kernel, ngx, ngy), out_shape=(vmem(state...  41.7 us

profile of v3, /device:TPU:1, one launch (start us, length us, event | category | flops | bytes accessed | tf_op | source)
XLA Modules:
  0.0 43.1 jit_solution(4487355973434712317)
XLA Ops:
  0.6 41.7 %film_step.1 = (f32[5,16,8,128]{3,2,1,0:T(8,128)S(1)}, f32[16,8,128]{2,1,0:T(8,128)S(1)}) custom-call(f32[5,16,8,128]{3,2,1,0:T(8,128)} %state_ref.1, f32[16,8,128]{2,1,0:T(8,128)} %pinning_ref.1, f32[2,8,128]{2,1,0:T(8,128)} %lead_ref.1, bf16[2,128,128]{2,1,0:T(8,128)(2,1)} %constant.12.clone.along_z_ref, bf16[2,64,256]{2,1,0:T(8,128)(2,1)} %constant.13.clone.along_x_ref, ...), custom_call_target="tpu_custom_call" | custom-call | tf_op jit(solution)/shard_map/film_step/pallas_call | solution.py:896
  42.3 0.8 %hand_over.1 = (f32[5,16,8,128]{3,2,1,0:T(8,128)}, f32[16,8,128]{2,1,0:T(8,128)}) custom-call(f32[5,16,8,128]{3,2,1,0:T(8,128)S(1)} %get-tuple-element.4.state_ref, f32[16,8,128]{2,1,0:T(8,128)S(1)} %get-tuple-element.5.potential_ref), custom_call_target="tpu_custom_call" | custom-call | tf_op jit(solution)/shard_map/hand_over/pallas_call | solution.py:965

commit v4 on v3

--- a/solution.py
+++ b/solution.py
@@ -81,7 +81,7 @@
         place = 2 * np.arange(ngx) + cell - 3
         within = (place >= 0) & (place < nx)
         along_x[:, within, cell] = tx[:, place[within]]
-    along_x = along_x.reshape(nx, ngx // 2, 2, 8).swapaxes(1, 2).reshape(nx, 8 * ngx)
+    along_x = np.moveaxis(along_x.reshape(nx, ngx // 2, 2, 8), 2, 0).reshape(2, nx, 4 * ngx)
     along_y = np.zeros((width, width))
     inverse = np.zeros((nx, width))
     values = (
@@ -215,6 +215,7 @@
         for dx in range(-2, 3)
         if (dx or dy) and abs(dx) * abs(dy) < 4 and (dx == 0 or abs(dy) < 4)
     ]
+    near.sort(key=lambda pair: abs(pair[0]) + abs(pair[1]))
     for dx, dy in near:
 
         @pl.when(within(dx, dy))
@@ -796,6 +797,9 @@
     each(0, TX, keep0)
     late0 = exchange0(1)
 
+    receive(near2)
+    unpack2()
+    smooth_down(level2, src2, va2, vb2)
     across.wait_recv()
     swap = pltpu.make_async_remote_copy(
         src_ref=gather2.at[core],
@@ -806,19 +810,28 @@
         device_id_type=MESH,
     )
     swap.start()
-    receive(near2)
-    unpack2()
-    smooth_down(level2, src2, va2, vb2)
+
+    def along_x_of(side):
+        shares = gather2[side].reshape(4 * ngx, 128 * groups)
+        return product((along_x[0, side], along_x[1, side]), halves(shares))
+
+    spectral = along_x_of(core)
     swap.wait_recv()
-    shares = gather2[...].reshape(8 * ngx, 128 * groups)
-    spectral = product((along_x[0], along_x[1]), halves(shares))
+    spectral = spectral + along_x_of(1 - core)
     spectral = product(halves(spectral), (along_y[0], along_y[1])) * inverse[...]
     spectral = product((back_x[0, :, : 2 * ngx], back_x[1, :, : 2 * ngx]), halves(spectral))
     spectral = halves(spectral)
-    for place in range(5):
-        column = product(spectral, (back_yz[0, place], back_yz[1, place]))
-        for x in range(6):
-            coarse[x, 2 * place + 2 : 2 * place + 4] = column[2 * x : 2 * x + 2]
+    for places in ((0, 1), (2, 3), (4,)):
+        back = [
+            jnp.concatenate([back_yz[part, place] for place in places], axis=1)
+            for part in range(2)
+        ]
+        columns = product(spectral, back)
+        for turn, place in enumerate(places):
+            for x in range(6):
+                coarse[x, 2 * place + 2 : 2 * place + 4] = columns[
+                    2 * x : 2 * x + 2, 128 * turn : 128 * turn + 128
+                ]
 
     smooth_up(
         level2,

time: 43.3 us -> 43.1 us (level)
  no operation moved by 1% of the time
where the time goes in v4:
time: 43.1 us; the launch traced here: 43 us
  Pallas kernels  42.3 us (98%)
  between operations  0.64 us (1%)
    pallas_call x1, Pallas kernels, body(): pl.pallas_call(functools.partial(kernel, ngx, ngy), out_shape=(vmem(state...  41.5 us

profile of v4, /device:TPU:1, one launch (start us, length us, event | category | flops | bytes accessed | tf_op | source)
XLA Modules:
  0.0 43.0 jit_solution(3645173990691656283)
XLA Ops:
  0.6 41.5 %film_step.1 = (f32[5,16,8,128]{3,2,1,0:T(8,128)S(1)}, f32[16,8,128]{2,1,0:T(8,128)S(1)}) custom-call(f32[5,16,8,128]{3,2,1,0:T(8,128)} %state_ref.1, f32[16,8,128]{2,1,0:T(8,128)} %pinning_ref.1, f32[2,8,128]{2,1,0:T(8,128)} %lead_ref.1, bf16[2,128,128]{2,1,0:T(8,128)(2,1)} %constant.12.clone.along_z_ref, ...), custom_call_target="tpu_custom_call" | custom-call | tf_op jit(solution)/shard_map/film_step/pallas_call | solution.py:909
  42.2 0.8 %hand_over.1 = (f32[5,16,8,128]{3,2,1,0:T(8,128)}, f32[16,8,128]{2,1,0:T(8,128)}) custom-call(f32[5,16,8,128]{3,2,1,0:T(8,128)S(1)} %get-tuple-element.4.state_ref, f32[16,8,128]{2,1,0:T(8,128)S(1)} %get-tuple-element.5.potential_ref), custom_call_target="tpu_custom_call" | custom-call | tf_op jit(solution)/shard_map/hand_over/pallas_call | solution.py:978

commit v5 on v4

--- a/solution.py
+++ b/solution.py
@@ -242,8 +242,10 @@
         )
     ]
     own_state.wait()
-    face_out[0] = ext[:, 1:17, 8:9, :]
-    face_out[1] = ext[:, 1:17, 15:16, :]
+    staged = (0, 1, 3, 2, 4)
+    for turn, field in enumerate(staged):
+        face_out[0, turn] = ext[field, 1:17, 8:9, :]
+        face_out[1, turn] = ext[field, 1:17, 15:16, :]
     pl.semaphore_wait(barrier, present)
 
     sent = []
@@ -267,12 +269,18 @@
             pl.when(inward)(lambda: copy.wait_recv())
 
     halo = [
-        push(face_out.at[0], face_in.at[0], 0, -1, halo_sem, 0),
-        push(face_out.at[1], face_in.at[1], 0, 1, halo_sem, 1),
-        push(ext.at[:, 1, 8:16], ext.at[:, 17, 8:16], -1, 0, halo_sem, 2),
-        push(ext.at[:, 16, 8:16], ext.at[:, 0, 8:16], 1, 0, halo_sem, 3),
-        push(face_out.at[1, 3, 0], diag_in.at[0], -1, 1, halo_sem, 4),
-        push(face_out.at[0, 2, 15], diag_in.at[1], 1, -1, halo_sem, 5),
+        push(face_out.at[0, 0:2], face_in.at[0, 0:2], 0, -1, halo_sem, 0),
+        push(face_out.at[1, 0:3], face_in.at[1, 0:3], 0, 1, halo_sem, 1),
+        push(ext.at[0:2, 1, 8:16], ext.at[0:2, 17, 8:16], -1, 0, halo_sem, 2),
+        push(ext.at[0:3, 16, 8:16], ext.at[0:3, 0, 8:16], 1, 0, halo_sem, 3),
+    ]
+    links = [
+        push(face_out.at[0, 2:5], face_in.at[0, 2:5], 0, -1, halo_sem, 4),
+        push(face_out.at[1, 3:5], face_in.at[1, 3:5], 0, 1, halo_sem, 5),
+        push(ext.at[2:5, 1, 8:16], ext.at[2:5, 17, 8:16], -1, 0, halo_sem, 6),
+        push(ext.at[3:5, 16, 8:16], ext.at[3:5, 0, 8:16], 1, 0, halo_sem, 7),
+        push(face_out.at[1, 2, 0], diag_in.at[0], -1, 1, halo_sem, 8),
+        push(face_out.at[0, 3, 15], diag_in.at[1], 1, -1, halo_sem, 9),
     ]
     for copy in locals_:
         copy.start()
@@ -398,26 +406,29 @@
     work[0, TX - 1] += jnp.where(gx == ngx - 1, 1.0, 0.0) * lead[1]
 
     receive(halo)
-    ext[:, 1:17, 16:17, :] = face_in[0]
-    ext[:, 1:17, 7:8, :] = face_in[1]
-    ext[3, 17, 7:8, :] = diag_in[0]
-    ext[2, 0, 16:17, :] = diag_in[1]
-
-    @pl.when(gx == 0)
-    def _():
-        ext[:, 0, :, :] = jnp.zeros((5, 24, NZ), jnp.float32)
-
-    @pl.when(gx == ngx - 1)
-    def _():
-        ext[:, 17, :, :] = jnp.zeros((5, 24, NZ), jnp.float32)
-
-    @pl.when(gy == 0)
-    def _():
-        ext[:, :, 7:8, :] = jnp.zeros((5, 18, 1, NZ), jnp.float32)
-
-    @pl.when(gy == ngy - 1)
-    def _():
-        ext[:, :, 16:17, :] = jnp.zeros((5, 18, 1, NZ), jnp.float32)
+    for turn, field in enumerate(staged[:3]):
+        if turn < 2:
+            ext[field, 1:17, 16:17, :] = face_in[0, turn]
+        ext[field, 1:17, 7:8, :] = face_in[1, turn]
+
+    def zero_outside():
+        @pl.when(gx == 0)
+        def _():
+            ext[:, 0, :, :] = jnp.zeros((5, 24, NZ), jnp.float32)
+
+        @pl.when(gx == ngx - 1)
+        def _():
+            ext[:, 17, :, :] = jnp.zeros((5, 24, NZ), jnp.float32)
+
+        @pl.when(gy == 0)
+        def _():
+            ext[:, :, 7:8, :] = jnp.zeros((5, 18, 1, NZ), jnp.float32)
+
+        @pl.when(gy == ngy - 1)
+        def _():
+            ext[:, :, 16:17, :] = jnp.zeros((5, 18, 1, NZ), jnp.float32)
+
+    zero_outside()
 
     def source_part(i, carry):
         from_re, from_im, from_current = carry
@@ -786,6 +797,14 @@
         rates[3, i] -= KAPPA2 * ((yz - (behind_z(yz) - under_y)) - (xy - flux_xy(i, -1, 0)))
         rates[4, i] -= KAPPA2 * ((zx - flux_zx(i, -1)) - (yz - flux_yz(i, -1)))
 
+    receive(links)
+    for turn, field in enumerate(staged[2:], 2):
+        ext[field, 1:17, 16:17, :] = face_in[0, turn]
+        if turn > 2:
+            ext[field, 1:17, 7:8, :] = face_in[1, turn]
+    ext[3, 17, 7:8, :] = diag_in[0]
+    ext[2, 0, 16:17, :] = diag_in[1]
+    zero_outside()
     each(0, TX, rate_part)
 
     def keep0(i):
@@ -962,7 +981,7 @@
                 vmem((2, ngx // 2, 8, width), f32),
                 dma((8,)),
                 dma,
-                dma((2, 6)),
+                dma((2, 10)),
                 dma((2, 2, 8)),
                 dma((2, 2, 8)),
                 dma((2, 14)),

time: 43.1 us -> 43.2 us (level)
  no operation moved by 1% of the time
where the time goes in v5:
time: 43.2 us; the launch traced here: 43.1 us
  Pallas kernels  42.4 us (98%)
  between operations  0.64 us (1%)
    pallas_call x1, Pallas kernels, body(): pl.pallas_call(functools.partial(kernel, ngx, ngy), out_shape=(vmem(state...  41.6 us

profile of v5, /device:TPU:1, one launch (start us, length us, event | category | flops | bytes accessed | tf_op | source)
XLA Modules:
  0.0 43.1 jit_solution(5631930985978105286)
XLA Ops:
  0.6 41.6 %film_step.1 = (f32[5,16,8,128]{3,2,1,0:T(8,128)S(1)}, f32[16,8,128]{2,1,0:T(8,128)S(1)}) custom-call(f32[5,16,8,128]{3,2,1,0:T(8,128)} %state_ref.1, f32[16,8,128]{2,1,0:T(8,128)} %pinning_ref.1, f32[2,8,128]{2,1,0:T(8,128)} %lead_ref.1, bf16[2,128,128]{2,1,0:T(8,128)(2,1)} %constant.12.clone.along_z_ref, ...), custom_call_target="tpu_custom_call" | custom-call | tf_op jit(solution)/shard_map/film_step/pallas_call | solution.py:928
  42.3 0.8 %hand_over.1 = (f32[5,16,8,128]{3,2,1,0:T(8,128)}, f32[16,8,128]{2,1,0:T(8,128)}) custom-call(f32[5,16,8,128]{3,2,1,0:T(8,128)S(1)} %get-tuple-element.4.state_ref, f32[16,8,128]{2,1,0:T(8,128)S(1)} %get-tuple-element.5.potential_ref), custom_call_target="tpu_custom_call" | custom-call | tf_op jit(solution)/shard_map/hand_over/pallas_call | solution.py:997

commit v6 on v5

--- a/solution.py
+++ b/solution.py
@@ -755,6 +755,22 @@
         gather2.at[core], chip, ngx // 2, lambda other: (2 * other + core, gy), 1
     )
 
+    def other_core(source, step):
+        return pltpu.make_async_remote_copy(
+            src_ref=source,
+            dst_ref=source,
+            send_sem=gather_sem.at[0, 2],
+            recv_sem=gather_sem.at[1, 2],
+            device_id=(2 * lax.rem(chip + step, ngx // 2) + 1 - core, gy),
+            device_id_type=MESH,
+        )
+
+    @pl.loop(0, ngx // 2)
+    def _(step):
+        other_core(gather2.at[core, chip], step).start()
+
+    swap = other_core(gather2.at[core], 0)
+
     receive(shared)
     total = share[1, 2]
     for dx, dy in around2:
@@ -820,16 +836,6 @@
     unpack2()
     smooth_down(level2, src2, va2, vb2)
     across.wait_recv()
-    swap = pltpu.make_async_remote_copy(
-        src_ref=gather2.at[core],
-        dst_ref=gather2.at[core],
-        send_sem=gather_sem.at[0, 2],
-        recv_sem=gather_sem.at[1, 2],
-        device_id=(gx + 1 - 2 * core, gy),
-        device_id_type=MESH,
-    )
-    swap.start()
-
     def along_x_of(side):
         shares = gather2[side].reshape(4 * ngx, 128 * groups)
         return product((along_x[0, side], along_x[1, side]), halves(shares))

time: 43.2 us -> 42.5 us (0.984)
  Pallas kernels: 42.4 us -> 41.7 us
    pallas_call x1, Pallas kernels: 41.6 us -> 40.9 us  [body(): pl.pallas_call(functools.partial(kernel, ngx, ngy), out_shape=(vmem(state...]
where the time goes in v6:
time: 42.5 us; the launch traced here: 42.3 us
  Pallas kernels  41.7 us (98%)
  between operations  0.64 us (2%)
    pallas_call x1, Pallas kernels, body(): pl.pallas_call(functools.partial(kernel, ngx, ngy), out_shape=(vmem(state...  40.9 us

profile of v6, /device:TPU:1, one launch (start us, length us, event | category | flops | bytes accessed | tf_op | source)
XLA Modules:
  0.0 42.3 jit_solution(6205428460495669103)
XLA Ops:
  0.6 40.9 %film_step.1 = (f32[5,16,8,128]{3,2,1,0:T(8,128)S(1)}, f32[16,8,128]{2,1,0:T(8,128)S(1)}) custom-call(f32[5,16,8,128]{3,2,1,0:T(8,128)} %state_ref.1, f32[16,8,128]{2,1,0:T(8,128)} %pinning_ref.1, f32[2,8,128]{2,1,0:T(8,128)} %lead_ref.1, bf16[2,128,128]{2,1,0:T(8,128)(2,1)} %constant.12.clone.along_z_ref, ...), custom_call_target="tpu_custom_call" | custom-call | tf_op jit(solution)/shard_map/film_step/pallas_call | solution.py:934
  41.5 0.8 %hand_over.1 = (f32[5,16,8,128]{3,2,1,0:T(8,128)}, f32[16,8,128]{2,1,0:T(8,128)}) custom-call(f32[5,16,8,128]{3,2,1,0:T(8,128)S(1)} %get-tuple-element.4.state_ref, f32[16,8,128]{2,1,0:T(8,128)S(1)} %get-tuple-element.5.potential_ref), custom_call_target="tpu_custom_call" | custom-call | tf_op jit(solution)/shard_map/hand_over/pallas_call | solution.py:1003
